TPU v7x, 512 devices: a whole 4x4x16 slice. The times are simulated.
512 devices in a mesh: dp: 4 (over x), expert: 32 (over y, z_hi, core), tensor: 4 (over z_lo).
Axes of the slice: x: 4, y: 4, z: 16 (z_hi: 4, z_lo: 4; z = z_hi * 4 + z_lo), core: 2. Of those that a mesh axis runs over, the one named last changes fastest.
Arguments:
- patches: bfloat16 [128, 576, 1280], P(('dp', 'expert'), None, 'tensor'), may hold values from -6 to 6
- router: bfloat16 [1280, 32], P('tensor'), may hold values from -0.15625 to 0.15625
- logits: float32 [128, 32, 576], P(('dp', 'expert')), may hold values from -16 to 260, as said below
- slot_outputs: bfloat16 [128, 32, 1280], P(('dp', 'expert'), None, 'tensor'), may hold values from -6 to 6
- cotangent: bfloat16 [128, 576, 1280], P(('dp', 'expert'), None, 'tensor'), may hold values from -6 to 6
- weight_in: bfloat16 [32, 1280, 5120], P('expert', None, ('dp', 'tensor')), may hold values from -0.15625 to 0.15625
- weight_out: bfloat16 [32, 5120, 1280], P('expert', ('dp', 'tensor')), may hold values from -0.078125 to 0.078125
Outputs:
- grad_patches: bfloat16 [128, 576, 1280], P(('dp', 'expert'), None, 'tensor')
- grad_router: float32 [1280, 32], P('tensor')
- grad_in: bfloat16 [32, 1280, 5120], P('expert', None, ('dp', 'tensor'))
- grad_out: bfloat16 [32, 5120, 1280], P('expert', ('dp', 'tensor'))
Inputs may be any that keep to these rules, and one draw needn't show every extreme that they name: Saved router logits; each row of either softmax has a finite largest entry.
All inputs are finite; a program needn't handle non-finite values.
Results may differ from a plain program's by a relative error of at most 0.0085.
Values may be sent and summed in bfloat16 or wider, within the bound.
No kernel may reach another device: no remote copies, remote signals or barrier semaphores. Data moves between devices by JAX's collectives and lax.ppermute only.
A program may use at most 64 MiB of HBM per device.

v0:
```python
import jax
import jax.numpy as jnp
from jax import lax
from jax.sharding import PartitionSpec as P


def softmax_backward(probs, upstream, axis):
    return probs * (upstream - jnp.sum(probs * upstream, axis=axis, keepdims=True))


def body(patches, router, logits, slot_outputs, cotangent, weight_in, weight_out):
    data_count = lax.axis_size("dp")
    tensor_count = lax.axis_size("tensor")
    width = patches.shape[2]
    hidden_dev = weight_in.shape[2]
    dispatch = jax.nn.softmax(logits, axis=2)
    combine = jax.nn.softmax(logits, axis=1)
    dispatch_low = dispatch.astype(jnp.bfloat16)
    combine_low = combine.astype(jnp.bfloat16)
    slot_inputs = jnp.einsum(
        "bsm,bmd->bsd", dispatch_low, patches, preferred_element_type=jnp.float32
    ).astype(jnp.bfloat16)
    slot_grads = jnp.einsum(
        "bsm,bmd->bsd", combine_low, cotangent, preferred_element_type=jnp.float32
    ).astype(jnp.bfloat16)
    moved_inputs, moved_grads = (
        lax.all_to_all(slot_inputs, "expert", split_axis=1, concat_axis=0, tiled=True),
        lax.all_to_all(slot_grads, "expert", split_axis=1, concat_axis=0, tiled=True),
    )
    rows_in, rows_grad = (
        lax.all_gather(moved_inputs, ("dp", "tensor"), axis=0, tiled=True),
        lax.all_gather(moved_grads, ("dp", "tensor"), axis=0, tiled=True),
    )
    expert_rows = rows_in.reshape(data_count, tensor_count, -1, width)
    expert_grads = rows_grad.reshape(data_count, tensor_count, -1, width)
    layout = "ptrd"
    first = weight_in[0].reshape(tensor_count, width, hidden_dev)
    second = weight_out[0].reshape(hidden_dev, tensor_count, width)
    before = jnp.einsum(
        layout + ",tdh->prh", expert_rows, first, preferred_element_type=jnp.float32
    )
    after, gelu_back = jax.vjp(jax.nn.gelu, before)
    after_low = after.astype(jnp.bfloat16)
    grad_after = jnp.einsum(
        layout + ",htd->prh", expert_grads, second, preferred_element_type=jnp.float32
    )
    grad_second = jnp.einsum(
        "prh," + layout + "->htd", after_low, expert_grads, preferred_element_type=jnp.float32
    )
    grad_second = grad_second.astype(jnp.bfloat16).reshape(1, hidden_dev, tensor_count * width)
    grad_before = gelu_back(grad_after)[0].astype(jnp.bfloat16)
    grad_first = jnp.einsum(
        layout + ",prh->tdh", expert_rows, grad_before, preferred_element_type=jnp.float32
    )
    grad_first = grad_first.astype(jnp.bfloat16).reshape(1, tensor_count * width, hidden_dev)
    partial_rows = jnp.einsum(
        "prh,tdh->ptrd", grad_before, first, preferred_element_type=jnp.float32
    )
    joined_rows = partial_rows.reshape(data_count * tensor_count, -1, width)
    summed = lax.psum_scatter(joined_rows, ("dp", "tensor"), scatter_dimension=0, tiled=True)
    returned = summed.reshape(-1, 1, width).astype(jnp.bfloat16)
    slot_back = lax.all_to_all(returned, "expert", split_axis=0, concat_axis=1, tiled=True)
    part_dispatch = jnp.einsum(
        "bsd,bmd->bsm", slot_back, patches, preferred_element_type=jnp.float32
    )
    part_combine = jnp.einsum(
        "bsd,bmd->bsm", slot_outputs, cotangent, preferred_element_type=jnp.float32
    )
    full_dispatch, full_combine = lax.psum((part_dispatch, part_combine), "tensor")
    grad_logits = softmax_backward(dispatch, full_dispatch, 2) + softmax_backward(
        combine, full_combine, 1
    )
    logit_low = grad_logits.astype(jnp.bfloat16)
    grad_patches = jnp.einsum(
        "bsm,bsd->bmd", dispatch_low, slot_back, preferred_element_type=jnp.float32
    )
    grad_patches = grad_patches + jnp.einsum(
        "bsm,ds->bmd", logit_low, router, preferred_element_type=jnp.float32
    )
    router_part = jnp.einsum("bmd,bsm->ds", patches, logit_low, preferred_element_type=jnp.float32)
    grad_router = lax.psum(router_part, ("dp", "expert"))
    return (grad_patches.astype(jnp.bfloat16), grad_router, grad_first, grad_second)


def solution(mesh):
    return jax.shard_map(
        body,
        mesh=mesh,
        in_specs=(
            P(("dp", "expert"), None, "tensor"),
            P("tensor", None),
            P(("dp", "expert"), None, None),
            P(("dp", "expert"), None, "tensor"),
            P(("dp", "expert"), None, "tensor"),
            P("expert", None, ("dp", "tensor")),
            P("expert", ("dp", "tensor"), None),
        ),
        out_specs=(
            P(("dp", "expert"), None, "tensor"),
            P("tensor", None),
            P("expert", None, ("dp", "tensor")),
            P("expert", ("dp", "tensor"), None),
        ),
        check_vma=False,
    )
```

profile of v0, /device:TPU:1, one launch (start us, length us, event | category | flops | bytes accessed | tf_op | source)
XLA Modules:
  0.0 1112.0 jit_solution(13928556427251955320)
XLA Ops:
  7.2 1.1 fusion.51
  8.3 1.1 fusion.30
  9.4 1.1 fusion.3
  10.6 0.5 broadcast.49
  11.1 0.8 reduce.6
  11.9 0.7 reshape.140
  12.6 19.4 %all-to-all-start.1 = ((bf16[32,2,160]{2,1,0:T(2,128)(2,1)}), bf16[32,2,160]{2,1,0:T(2,128)(2,1)S(1)}, u32[]{:S(2)}, u32[]{:S(2)}) async-start(bf16[32,2,160]{2,1,0:T(2,128)(2,1)} %reshape.140), calls=%async_computation.1 | async-start | bytes 65536 | tf_op jit(solution)/shard_map/all_to_all | solution.py:27
  32.0 0.6 copy.42
  33.0 0.8 reduce.7
  33.8 0.7 reshape.142
  34.5 2.5 reshape_squeeze.6
  37.0 9.5 all-to-all-done.1
  46.5 5.1 all-to-all-start
  51.8 38.2 %all-gather.1 = bf16[1,512,320]{2,1,0:T(8,128)(2,1)S(1)} all-gather(bf16[1,32,320]{2,1,0:T(8,128)(2,1)S(1)} %copy.31), channel_id=3, replica_groups=mesh['dp'=4,'expert'=32,'tensor'=4] {'dp','tensor'}, dimensions={1}, use_global_device_ids=true | all-gather | bytes 348160 | tf_op jit(solution)/shard_map/all_gather | solution.py:31
  90.1 33.6 %all-gather = bf16[1,512,320]{2,1,0:T(8,128)(2,1)S(1)} all-gather(bf16[1,32,320]{2,1,0:T(8,128)(2,1)S(1)} %copy.28), channel_id=2, replica_groups=mesh['dp'=4,'expert'=32,'tensor'=4] {'dp','tensor'}, dimensions={1}, use_global_device_ids=true | all-gather | bytes 348160 | tf_op jit(solution)/shard_map/all_gather | solution.py:32
  124.1 0.5 fusion.20
  124.6 1.4 fusion.52
  126.0 0.8 convolution_bitcast_fusion.2
  127.3 89.6 %reduce-scatter.2.cloned.1.call-done = f32[1,32,320]{2,1,0:T(8,128)} async-done(((f32[16,32,320]{2,1,0:T(8,128)}), f32[1,32,320]{2,1,0:T(8,128)}) %reduce-scatter.2.cloned.1.call-update) | async-done | bytes 40976 | tf_op jit(solution)/shard_map/reduce_scatter | solution.py:60
  216.9 0.8 convert_bitcast_fusion
  217.7 0.7 reduce.8
  218.4 0.7 reshape.144
  219.1 24.1 %all-to-all-start.2 = ((bf16[32,2,160]{2,1,0:T(2,128)(2,1)}), bf16[32,2,160]{2,1,0:T(2,128)(2,1)S(1)}, u32[]{:S(2)}, u32[]{:S(2)}) async-start(bf16[32,2,160]{2,1,0:T(2,128)(2,1)} %reshape.144), calls=%async_computation.3 | async-start | bytes 65536 | tf_op jit(solution)/shard_map/all_to_all | solution.py:62
  243.7 1.3 copy.36
  245.0 1.3 copy.37
  246.2 11.4 %all-to-all-done.2 = bf16[32,2,160]{2,1,0:T(2,128)(2,1)S(1)} async-done(((bf16[32,2,160]{2,1,0:T(2,128)(2,1)}), bf16[32,2,160]{2,1,0:T(2,128)(2,1)S(1)}, u32[]{:S(2)}, u32[]{:S(2)}) %all-to-all-start.2) | async-done | bytes 20512 | tf_op jit(solution)/shard_map/all_to_all | solution.py:62
  257.7 0.8 convolution_bitcast_fusion.3
  258.9 46.1 %all-reduce.3.cloned.1.call-done = (f32[1,32,576]{2,1,0:T(8,128)}, f32[1,32,576]{2,1,0:T(8,128)}) async-done(((f32[1,32,576]{2,1,0:T(8,128)}, f32[1,32,576]{2,1,0:T(8,128)}), (f32[1,32,576]{2,1,0:T(8,128)}, f32[1,32,576]{2,1,0:T(8,128)})) %all-reduce.3.cloned.1.call-update) | async-done | bytes 147472 | tf_op jit(solution)/shard_map/psum | solution.py:69
  305.0 1.1 multiply_reduce_fusion.1
  306.1 1.0 fusion.31
  307.4 796.6 %psum.23 = f32[320,32]{0,1:T(8,128)} all-reduce(f32[320,32]{0,1:T(8,128)S(1)} %convolution_bitcast_fusion.4), channel_id=1, replica_groups=mesh['dp'=4,'expert'=32,'tensor'=4] {'dp','expert'}, use_global_device_ids=true, to_apply=%region_9.0 | all-reduce | flops 10240 | bytes 81920 | tf_op jit(solution)/shard_map/psum | solution.py:81
  1104.1 1.1 fusion.1
  (32 shorter events, 2.6 us)
Async XLA Ops:
  7.2 2.2 copy-start
  7.2 24.9 %copy-start.2 = (bf16[1,1280,320]{1,2,0:T(8,128)(2,1)S(1)}, bf16[1,1280,320]{1,2,0:T(8,128)(2,1)}, u32[]{:S(2)}) copy-start(bf16[1,1280,320]{1,2,0:T(8,128)(2,1)} %param.12) | copy-start | bytes 2457604
  11.1 21.6 %copy-start.1 = (f32[1,32,576]{2,1,0:T(8,128)S(1)}, f32[1,32,576]{2,1,0:T(8,128)}, u32[]{:S(2)}) copy-start(f32[1,32,576]{2,1,0:T(8,128)} %param.9) | copy-start | bytes 221188
  11.1 21.6 %copy-start.3 = (bf16[1,576,320]{1,2,0:T(8,128)(2,1)S(1)}, bf16[1,576,320]{1,2,0:T(8,128)(2,1)}, u32[]{:S(2)}) copy-start(bf16[1,576,320]{1,2,0:T(8,128)(2,1)} %param.11) | copy-start | bytes 1105924
  12.6 33.9 %all-to-all-start.1 = ((bf16[32,2,160]{2,1,0:T(2,128)(2,1)}), bf16[32,2,160]{2,1,0:T(2,128)(2,1)S(1)}, u32[]{:S(2)}, u32[]{:S(2)}) async-start(bf16[32,2,160]{2,1,0:T(2,128)(2,1)} %reshape.140), calls=%async_computation.1 | async-start | bytes 65536 | tf_op jit(solution)/shard_map/all_to_all | solution.py:27
  46.5 43.5 %all-to-all-start = ((bf16[32,2,160]{2,1,0:T(2,128)(2,1)}), bf16[32,2,160]{2,1,0:T(2,128)(2,1)S(1)}, u32[]{:S(2)}, u32[]{:S(2)}) async-start(bf16[32,2,160]{2,1,0:T(2,128)(2,1)} %reshape.142), calls=%async_computation | async-start | bytes 65536 | tf_op jit(solution)/shard_map/all_to_all | solution.py:28
  51.7 165.3 %reduce-scatter.2.cloned.1.call-start = ((), (), s32[]{:S(2)}) async-start(), calls=%async_computation.4 | async-start | bytes 835584 | tf_op jit(solution)/shard_map/reduce_scatter | solution.py:60
  124.6 1.4 copy-start.4
  124.6 1.4 copy-start.5
  219.1 38.5 %all-to-all-start.2 = ((bf16[32,2,160]{2,1,0:T(2,128)(2,1)}), bf16[32,2,160]{2,1,0:T(2,128)(2,1)S(1)}, u32[]{:S(2)}, u32[]{:S(2)}) async-start(bf16[32,2,160]{2,1,0:T(2,128)(2,1)} %reshape.144), calls=%async_computation.3 | async-start | bytes 65536 | tf_op jit(solution)/shard_map/all_to_all | solution.py:62
  243.2 61.8 %all-reduce.3.cloned.1.call-start = ((), (), s32[]{:S(2)}) async-start(), calls=%async_computation.5 | async-start | bytes 327680 | tf_op jit(solution)/shard_map/psum | solution.py:69
  258.6 845.5 %copy-start.6 = (bf16[320,32]{0,1:T(8,128)(2,1)S(1)}, bf16[320,32]{0,1:T(8,128)(2,1)}, u32[]{:S(2)}) copy-start(bf16[320,32]{0,1:T(8,128)(2,1)} %param.8) | copy-start | bytes 61444
Sparse Core Ops, SparseCore 0:
  126.1 90.7 reduce-scatter.1
  258.7 46.2 all-reduce.2
where the time goes:
time: 1120 us; the launch traced here: 1110 us
  blocking collectives  868 us (78%)
  waiting for transfers between devices  157 us (14%)
  starting transfers between devices  48.7 us (4%)
  between operations  14.3 us (1%)
    psum x1, blocking collectives, body(): grad_router = lax.psum(router_part, ('dp', 'expert'))  797 us
    reduce_scatter x1, waiting for transfers between devices, body(): lax.psum_scatter(joined_rows, ('dp', 'tensor'), scatter_dimension=0, tile...  89.6 us
    psum x1, waiting for transfers between devices, body(): lax.psum((part_dispatch, part_combine), 'tensor')  46.1 us
    all_gather x1, blocking collectives, body(): lax.all_gather(moved_inputs, ('dp', 'tensor'), axis=0, tiled=True)  38.2 us
    all_gather x1, blocking collectives, body(): lax.all_gather(moved_grads, ('dp', 'tensor'), axis=0, tiled=True)  33.6 us
    all_to_all x1, starting transfers between devices, body(): lax.all_to_all(returned, 'expert', split_axis=0, concat_axis=1, tiled=True)  24.1 us
  transfers between devices with their start and end apart: 5, of which 4 were waited for; matrix products, arithmetic and copies ran while one was open for 1% of the time, Pallas kernels for 0%

commit v1 on v0

v1 whole, which is shorter than its diff:
```python
import jax
import jax.numpy as jnp
from jax import lax
from jax.experimental import pallas as pl
from jax.experimental.pallas import tpu as pltpu
from jax.sharding import Mesh
from jax.sharding import PartitionSpec as P

F32 = jnp.float32
BF16 = jnp.bfloat16
RING = ("zh", "tensor")
PLANE = ("dp", "y", "core")
COLUMN = ("y", "core")
CROSS = ("dp", "zh")


def call(kernel, outs, *args):
    return pl.pallas_call(
        kernel,
        out_shape=outs,
        compiler_params=pltpu.CompilerParams(vmem_limit_bytes=48 * 1024 * 1024),
    )(*args)


def shape(dims, dtype):
    return jax.ShapeDtypeStruct(dims, dtype)


def pieces():
    return [(8 * zh + 2 * y, 8 * y + 2 * zh) for zh in range(4) for y in range(4)]


def rounded_dot(a, b, dims):
    return lax.dot_general(a, b, (dims, ((), ())), preferred_element_type=F32)


def image_kernel(logits, patches, cotangent, saved, send, dispatch, combine, grad_combine):
    for new, old in pieces():
        dispatch[new : new + 2, :] = logits[0, old : old + 2, :]
    values = dispatch[...]
    top = jnp.exp(values - jnp.max(values, axis=1, keepdims=True))
    by_patch = top / jnp.sum(top, axis=1, keepdims=True)
    low = jnp.exp(values - jnp.max(values, axis=0, keepdims=True))
    by_slot = low / jnp.sum(low, axis=0, keepdims=True)
    dispatch[...] = by_patch
    combine[...] = by_slot
    slot_in = jnp.dot(by_patch.astype(BF16), patches[0], preferred_element_type=F32)
    slot_grad = jnp.dot(by_slot.astype(BF16), cotangent[0], preferred_element_type=F32)
    width = slot_in.shape[1]
    for zh in range(4):
        ins = slot_in[8 * zh : 8 * zh + 8, :].astype(BF16)
        grads = slot_grad[8 * zh : 8 * zh + 8, :].astype(BF16)
        for zl in range(4):
            send[4 * zh + zl, :, 0:width] = ins
            send[4 * zh + zl, :, width : 2 * width] = grads
    part = rounded_dot(saved[0], cotangent[0], ((1,), (1,)))
    for new, old in pieces():
        grad_combine[new : new + 2, :] = part[old : old + 2, :]


def regroup_kernel(got, send, stage):
    width = got.shape[2] // 2
    for zh in range(4):
        for zl in range(4):
            block = got[4 * zh + zl].astype(F32)
            for kind in range(2):
                row = 32 * kind + 8 * zh
                stage[row : row + 8, width * zl : width * (zl + 1)] = block[
                    :, width * kind : width * (kind + 1)
                ]
    row = lax.broadcasted_iota(jnp.int32, (64, 64), 0)
    col = lax.broadcasted_iota(jnp.int32, (64, 64), 1)
    move = (row == (col % 8) * 8 + col // 8).astype(F32).astype(BF16)
    moved = jnp.dot(move, stage[...].astype(BF16), preferred_element_type=F32).astype(BF16)
    for x in range(4):
        send[8 * x : 8 * x + 8] = moved.reshape(8, 8, 4 * width)


GELU_SCALE = 0.7978845608028654
GELU_CUBE = 0.044715


def expert_kernel(rows, first, second, send, grad_before, after):
    both = rows[...].reshape(256, rows.shape[2])
    before = jnp.dot(both, first[0], preferred_element_type=F32)
    grad_after = rounded_dot(both, second[0], ((1,), (1,)))
    grad_after = pltpu.roll(grad_after, 252, 0)
    is_in = lax.broadcasted_iota(jnp.int32, before.shape, 0) % 8 < 4
    square = before * before
    bent = jnp.tanh(GELU_SCALE * (before + GELU_CUBE * (before * square)))
    half = 0.5 * (1.0 + bent)
    slope = half + before * (
        (0.5 * GELU_SCALE) * ((1.0 - bent) * (1.0 + bent)) * (1.0 + (3.0 * GELU_CUBE) * square)
    )
    grads = jnp.where(is_in, grad_after * slope, 0.0)
    low = grads.astype(BF16)
    shifted = pltpu.roll(grads, 4, 0).astype(BF16)
    part = first.shape[1] // 2
    total = rounded_dot(low, first[0, :part, :], ((1,), (1,)))
    total = total + rounded_dot(shifted, first[0, part:, :], ((1,), (1,)))
    send[...] = total.astype(BF16).reshape(send.shape)
    grad_before[...] = low
    after[...] = pltpu.roll(jnp.where(is_in, before * half, 0.0), 4, 0).astype(BF16)


def weight_kernel(rows, grad_before, after, grad_first, grad_second):
    both = rows[...].reshape(256, rows.shape[2])
    grad_first[0] = rounded_dot(both, grad_before[...], ((0,), (0,))).astype(BF16)
    grad_second[0] = rounded_dot(after[...], both, ((0,), (0,))).astype(BF16)


def partial_kernel(got, send):
    total = got[0:8].astype(F32)
    for x in range(1, 4):
        total = total + got[8 * x : 8 * x + 8].astype(F32)
    low = total.reshape(64, got.shape[2]).astype(BF16)
    row = lax.broadcasted_iota(jnp.int32, (64, 64), 0)
    col = lax.broadcasted_iota(jnp.int32, (64, 64), 1)
    move = (row == (col % 8) * 8 + col // 8).astype(F32).astype(BF16)
    moved = jnp.dot(move, low, preferred_element_type=F32).astype(BF16)
    width = send.shape[2]
    for zh in range(4):
        for zl in range(4):
            at = (zl // 2) * 32 + 8 * zh
            lane = (zl % 2) * width
            send[4 * zh + zl] = moved[at : at + 8, lane : lane + width]


def back_kernel(got, patches, grad_combine, send, slot_back):
    for zh in range(4):
        total = got[4 * zh].astype(F32)
        for zl in range(1, 4):
            total = total + got[4 * zh + zl].astype(F32)
        slot_back[8 * zh : 8 * zh + 8, :] = total
    low = slot_back[...].astype(BF16)
    part = rounded_dot(low, patches[0], ((1,), (1,)))
    both = jnp.concatenate([part, grad_combine[...]], axis=0).astype(BF16)
    for zl in range(4):
        send[zl] = both


def logit_kernel(got, dispatch, combine, patches, grad_logits, send):
    total = got[0].astype(F32)
    for zl in range(1, 4):
        total = total + got[zl].astype(F32)
    by_patch, by_slot = dispatch[...], combine[...]
    up, down = total[:32], total[32:]
    grads = by_patch * (up - jnp.sum(by_patch * up, axis=1, keepdims=True))
    grads = grads + by_slot * (down - jnp.sum(by_slot * down, axis=0, keepdims=True))
    low = grads.astype(BF16)
    grad_logits[...] = low
    router = jnp.dot(low, patches[0], preferred_element_type=F32)
    width = send.shape[2]
    for j in range(8):
        lane = (j // 4) * width
        send[j] = router[(j % 4) * 8 : (j % 4) * 8 + 8, lane : lane + width]


def patch_kernel(dispatch, slot_back, grad_logits, router, grad_patches):
    new = lax.broadcasted_iota(jnp.int32, (32, 32), 0)
    old = lax.broadcasted_iota(jnp.int32, (32, 32), 1)
    move = (old == ((new // 2) % 4) * 8 + (new // 8) * 2 + new % 2).astype(F32).astype(BF16)
    columns = rounded_dot(move, router[...], ((1,), (1,))).astype(BF16)
    left = jnp.concatenate([dispatch[...], grad_logits[...].astype(F32)], axis=0).astype(BF16)
    right = jnp.concatenate([slot_back[...], columns.astype(F32)], axis=0).astype(BF16)
    grad_patches[0] = rounded_dot(left, right, ((0,), (0,))).astype(BF16)


def exchange(value, axes):
    return lax.all_to_all(value, axes, 0, 0, tiled=True)


def summed(value, axes, count):
    copies = jnp.broadcast_to(value[None], (count,) + value.shape)
    return jnp.sum(exchange(copies, axes), axis=0)


def body(patches, router, logits, slot_outputs, cotangent, weight_in, weight_out):
    count, width = patches.shape[1:]
    deep = weight_in.shape[1]
    hidden = weight_in.shape[2]
    send, dispatch, combine, grad_combine = call(
        image_kernel,
        [
            shape((16, 8, 2 * width), BF16),
            shape((32, count), F32),
            shape((32, count), F32),
            shape((32, count), F32),
        ],
        logits,
        patches,
        cotangent,
        slot_outputs,
    )
    got = exchange(send, RING)
    send = pl.pallas_call(
        regroup_kernel,
        out_shape=shape((32, 8, deep), BF16),
        scratch_shapes=[pltpu.VMEM((64, deep), F32)],
    )(got)
    rows = exchange(send, PLANE)
    send, grad_before, after = call(
        expert_kernel,
        [
            shape((32, 8, deep // 2), BF16),
            shape((256, hidden), BF16),
            shape((256, hidden), BF16),
        ],
        rows,
        weight_in,
        weight_out,
    )
    got = exchange(send, PLANE)
    grad_first, grad_second = call(
        weight_kernel,
        [shape((1, deep, hidden), BF16), shape((1, hidden, deep), BF16)],
        rows,
        grad_before,
        after,
    )
    send = call(partial_kernel, shape((16, 8, width), BF16), got)
    got = exchange(send, RING)
    send, slot_back = call(
        back_kernel,
        [shape((4, 64, count), BF16), shape((32, width), F32)],
        got,
        patches,
        grad_combine,
    )
    got = exchange(send, "tensor")
    grad_logits, send = call(
        logit_kernel,
        [shape((32, count), BF16), shape((8, 8, width // 2), F32)],
        got,
        dispatch,
        combine,
        patches,
    )
    own = jnp.sum(exchange(send, COLUMN), axis=0)
    grad_patches = call(
        patch_kernel,
        shape((1, count, width), BF16),
        dispatch,
        slot_back,
        grad_logits,
        router,
    )
    own = summed(own, CROSS, 16)
    whole = exchange(jnp.broadcast_to(own[None], (8,) + own.shape), COLUMN)
    whole = whole.reshape(2, 4, 4, 2, width // 2)
    grad_router = jnp.transpose(whole, (0, 4, 2, 1, 3)).reshape(width, 32)
    return (grad_patches, grad_router, grad_first, grad_second)


def solution(mesh):
    split = Mesh(mesh.devices.reshape(4, 4, 4, 2, 4), ("dp", "y", "zh", "core", "tensor"))
    images = ("dp", "y", "zh", "core")
    experts = ("y", "zh", "core")
    return jax.shard_map(
        body,
        mesh=split,
        in_specs=(
            P(images, None, "tensor"),
            P("tensor", None),
            P(images, None, None),
            P(images, None, "tensor"),
            P(images, None, "tensor"),
            P(experts, None, ("dp", "tensor")),
            P(experts, ("dp", "tensor"), None),
        ),
        out_specs=(
            P(images, None, "tensor"),
            P("tensor", None),
            P(experts, None, ("dp", "tensor")),
            P(experts, ("dp", "tensor"), None),
        ),
        check_vma=False,
    )
```

time: 1120 us -> 144 us (0.13)
  blocking collectives: 868 us -> 100 us
  waiting for transfers between devices: 157 us -> 11.7 us
  starting transfers between devices: 48.7 us -> 16.4 us
  between operations: 14.3 us -> 0.74 us
    psum x1 -> x0, blocking collectives: 797 us -> none  [body(): grad_router = lax.psum(router_part, ('dp', 'expert'))]
    all_to_all x0 -> x6, blocking collectives: none -> 100 us  [exchange(): return lax.all_to_all(value, axes, 0, 0, tiled=True)]
    reduce_scatter x1 -> x0, waiting for transfers between devices: 89.6 us -> none  [body(): lax.psum_scatter(joined_rows, ('dp', 'tensor'), scatter_dimension=0, tile...]
    all_gather x2 -> x0, blocking collectives: 71.8 us -> none  [the longest x1 38.2 us: body(): lax.all_gather(moved_inputs, ('dp', 'tensor'), axis=0, tiled=True)]
    psum x1 -> x0, waiting for transfers between devices: 46.1 us -> none  [body(): lax.psum((part_dispatch, part_combine), 'tensor')]
    all_to_all x3 -> x2, starting transfers between devices: 48.6 us -> 16.4 us  [exchange(): return lax.all_to_all(value, axes, 0, 0, tiled=True)]
  transfers between devices with their start and end apart: 5 -> 2, of which waited for: 4 -> 2; matrix products, arithmetic and copies ran while one was open for 1% -> 3% of each run, Pallas kernels for 0% -> 1%
where the time goes in v1:
time: 144 us
  blocking collectives  100 us (69%)
  starting transfers between devices  16.4 us (11%)
  waiting for transfers between devices  11.7 us (8%)
  local copies, waits for them, and re-layouts  7.61 us (5%)
  Pallas kernels  6.92 us (5%)
    all_to_all x6, blocking collectives, exchange(): return lax.all_to_all(value, axes, 0, 0, tiled=True)  100 us
    all_to_all x2, starting transfers between devices, exchange(): return lax.all_to_all(value, axes, 0, 0, tiled=True)  16.4 us
    all_to_all x2, waiting for transfers between devices, exchange(): return lax.all_to_all(value, axes, 0, 0, tiled=True)  11.7 us
    unnamed x16, local copies, waits for them, and re-layouts  6.14 us
    pallas_call x7, Pallas kernels, call(): pl.pallas_call(kernel, out_shape=outs, compiler_params=pltpu.CompilerPara...  4.91 us
  transfers between devices with their start and end apart: 2, of which 2 were waited for; matrix products, arithmetic and copies ran while one was open for 3% of the time, Pallas kernels for 1%

profile of v1, /device:TPU:1, one launch (start us, length us, event | category | flops | bytes accessed | tf_op | source)
XLA Modules:
  0.0 143.6 jit_solution(9202371549978372340)
XLA Ops:
  0.6 1.3 copy.36.patches
  1.9 0.0 copy-done.3
  1.9 0.0 copy-start.1
  2.0 0.0 copy-start.2
  2.0 0.2 copy.37.cotangent
  2.2 0.6 copy-done.1
  2.8 0.6 shard_map.102
  3.4 27.9 %all_to_all.40.got = bf16[16,8,640]{2,1,0:T(8,128)(2,1)} all-to-all(bf16[16,8,640]{2,1,0:T(8,128)(2,1)S(1)} %get-tuple-element.18), channel_id=1, replica_groups=mesh['dp'=4,'y'=4,'zh'=4,'core'=2,'tensor'=4] {'zh','tensor'}, dimensions={0} | all-to-all | bytes 327680 | tf_op jit(solution)/shard_map/all_to_all | solution.py:170
  31.3 2.0 %shard_map.103 = bf16[32,8,1280]{2,1,0:T(8,128)(2,1)} custom-call(bf16[16,8,640]{2,1,0:T(8,128)(2,1)} %all_to_all.40.got), custom_call_target="tpu_custom_call" | custom-call | tf_op jit(solution)/shard_map/pallas_call | solution.py:196
  33.3 11.5 %all-to-all-start.1 = ((bf16[32,8,1280]{2,1,0:T(8,128)(2,1)}), bf16[32,8,1280]{2,1,0:T(8,128)(2,1)S(1)}, u32[]{:S(2)}, u32[]{:S(2)}) async-start(bf16[32,8,1280]{2,1,0:T(8,128)(2,1)} %shard_map.103), calls=%async_computation.1 | async-start | bytes 1310720 | tf_op jit(solution)/shard_map/all_to_all | solution.py:170
  44.7 0.0 copy-start
  44.8 1.6 %copy.38.first = bf16[1,1280,320]{2,1,0:T(8,128)(2,1)S(1)} copy(bf16[1,1280,320]{1,2,0:T(8,128)(2,1)} %param.12) | data formatting | bytes 1638400 | tf_op args[5]
  46.4 11.3 %all-to-all-done.1.rows = bf16[32,8,1280]{2,1,0:T(8,128)(2,1)S(1)} async-done(((bf16[32,8,1280]{2,1,0:T(8,128)(2,1)}), bf16[32,8,1280]{2,1,0:T(8,128)(2,1)S(1)}, u32[]{:S(2)}, u32[]{:S(2)}) %all-to-all-start.1) | async-done | bytes 655392 | tf_op jit(solution)/shard_map/all_to_all | solution.py:170
  57.7 1.5 %shard_map.104 = (bf16[32,8,640]{2,1,0:T(8,128)(2,1)S(1)}, bf16[256,320]{1,0:T(8,128)(2,1)S(1)}, bf16[256,320]{1,0:T(8,128)(2,1)S(1)}) custom-call(bf16[32,8,1280]{2,1,0:T(8,128)(2,1)S(1)} %all-to-all-done.1.rows, bf16[1,1280,320]{2,1,0:T(8,128)(2,1)S(1)} %copy.38.first, bf16[1,320,1280]{2,1,0:T(8,128)(2,1)S(1)} %copy-done), custom_call_target="tpu_custom_call" | custom-call | tf_op jit(solution)/shard_map/pallas_call | solution.py:18
  59.1 13.2 %all_to_all.41.got = bf16[32,8,640]{2,1,0:T(8,128)(2,1)S(1)} all-to-all(bf16[32,8,640]{2,1,0:T(8,128)(2,1)S(1)} %get-tuple-element.19), channel_id=1, replica_groups=mesh['dp'=4,'y'=4,'zh'=4,'core'=2,'tensor'=4] {'dp','y','core'}, dimensions={0} | all-to-all | bytes 655360 | tf_op jit(solution)/shard_map/all_to_all | solution.py:170
  72.3 0.3 shard_map.105
  72.6 15.7 %all_to_all.42.got = bf16[16,8,320]{2,1,0:T(8,128)(2,1)S(1)} all-to-all(bf16[16,8,320]{2,1,0:T(8,128)(2,1)S(1)} %shard_map.105), channel_id=1, replica_groups=mesh['dp'=4,'y'=4,'zh'=4,'core'=2,'tensor'=4] {'zh','tensor'}, dimensions={0} | all-to-all | bytes 163840 | tf_op jit(solution)/shard_map/all_to_all | solution.py:170
  88.3 0.3 shard_map.106
  88.6 13.0 %all_to_all.43.got = bf16[4,64,576]{2,1,0:T(8,128)(2,1)S(1)} all-to-all(bf16[4,64,576]{2,1,0:T(8,128)(2,1)S(1)} %get-tuple-element.22), channel_id=1, replica_groups=mesh['dp'=4,'y'=4,'zh'=4,'core'=2,'tensor'=4] {'tensor'}, dimensions={0} | all-to-all | bytes 589824 | tf_op jit(solution)/shard_map/all_to_all | solution.py:170
  101.6 0.3 shard_map.107
  101.9 9.6 %all_to_all.44 = f32[8,8,160]{2,1,0:T(8,128)S(1)} all-to-all(f32[8,8,160]{2,1,0:T(8,128)S(1)} %get-tuple-element.25), channel_id=1, replica_groups=mesh['dp'=4,'y'=4,'zh'=4,'core'=2,'tensor'=4] {'y','core'}, dimensions={0} | all-to-all | bytes 81920 | tf_op jit(solution)/shard_map/all_to_all | solution.py:170
  111.5 20.8 %all_to_all.45 = f32[16,8,160]{2,1,0:T(8,128)S(1)} all-to-all(f32[16,8,160]{2,1,0:T(8,128)S(1)} %broadcast_in_dim.4), channel_id=1, replica_groups=mesh['dp'=4,'y'=4,'zh'=4,'core'=2,'tensor'=4] {'dp','zh'}, dimensions={0} | all-to-all | bytes 163840 | tf_op jit(solution)/shard_map/all_to_all | solution.py:170
  132.3 0.6 broadcast_in_dim.5
  133.0 5.0 %all-to-all-start.7 = ((f32[8,8,160]{2,1,0:T(8,128)}), f32[8,8,160]{2,1,0:T(8,128)S(1)}, u32[]{:S(2)}, u32[]{:S(2)}) async-start(f32[8,8,160]{2,1,0:T(8,128)} %broadcast_in_dim.5), calls=%async_computation.7 | async-start | bytes 131072 | tf_op jit(solution)/shard_map/all_to_all | solution.py:170
  137.9 0.1 copy.41.router
  138.1 1.7 %shard_map.109 = (bf16[1,1280,320]{2,1,0:T(8,128)(2,1)S(1)}, bf16[1,320,1280]{2,1,0:T(8,128)(2,1)}) custom-call(bf16[32,8,1280]{2,1,0:T(8,128)(2,1)S(1)} %all-to-all-done.1.rows, bf16[256,320]{1,0:T(8,128)(2,1)S(1)} %get-tuple-element.26.grad_before, bf16[256,320]{1,0:T(8,128)(2,1)S(1)} %get-tuple-element.27.after), custom_call_target="tpu_custom_call" | custom-call | tf_op jit(solution)/shard_map/pallas_call | solution.py:18
  139.7 1.3 copy.44
  141.0 0.4 shard_map.108
  141.4 1.0 copy.43
  142.3 0.4 all-to-all-done.7
  142.8 0.1 copy.42
  142.9 0.7 reshape.17
  (9 shorter events, 0.1 us)
Async XLA Ops:
  0.6 1.3 copy-start.3
  1.9 0.9 copy-start.1
  2.0 0.9 copy-start.2
  33.3 24.4 %all-to-all-start.1 = ((bf16[32,8,1280]{2,1,0:T(8,128)(2,1)}), bf16[32,8,1280]{2,1,0:T(8,128)(2,1)S(1)}, u32[]{:S(2)}, u32[]{:S(2)}) async-start(bf16[32,8,1280]{2,1,0:T(8,128)(2,1)} %shard_map.103), calls=%async_computation.1 | async-start | bytes 1310720 | tf_op jit(solution)/shard_map/all_to_all | solution.py:170
  44.7 12.9 %copy-start = (bf16[1,320,1280]{2,1,0:T(8,128)(2,1)S(1)}, bf16[1,320,1280]{2,1,0:T(8,128)(2,1)}, u32[]{:S(2)}) copy-start(bf16[1,320,1280]{2,1,0:T(8,128)(2,1)} %second.1) | copy-start | bytes 2457604
  133.0 5.0 %copy-start.4 = (bf16[320,32]{0,1:T(8,128)(2,1)S(1)}, bf16[320,32]{0,1:T(8,128)(2,1)}, u32[]{:S(2)}) copy-start(bf16[320,32]{0,1:T(8,128)(2,1)} %param.8) | copy-start | bytes 61444
  133.0 9.8 %all-to-all-start.7 = ((f32[8,8,160]{2,1,0:T(8,128)}), f32[8,8,160]{2,1,0:T(8,128)S(1)}, u32[]{:S(2)}, u32[]{:S(2)}) async-start(f32[8,8,160]{2,1,0:T(8,128)} %broadcast_in_dim.5), calls=%async_computation.7 | async-start | bytes 131072 | tf_op jit(solution)/shard_map/all_to_all | solution.py:170

commit v2 on v1

v2 whole, which is shorter than its diff:
```python
import jax
import jax.numpy as jnp
from jax import lax
from jax.experimental import pallas as pl
from jax.experimental.pallas import tpu as pltpu
from jax.sharding import Mesh
from jax.sharding import PartitionSpec as P

F32 = jnp.float32
BF16 = jnp.bfloat16
RING = ("zh", "tensor")
PLANE = ("dp", "y", "core")
SHEET = ("dp", "y")
LINE = ("zh", "core")


def call(kernel, outs, *args, scratch=()):
    return pl.pallas_call(
        kernel,
        out_shape=outs,
        scratch_shapes=scratch,
        compiler_params=pltpu.CompilerParams(vmem_limit_bytes=24 * 1024 * 1024),
    )(*args)


def shape(dims, dtype):
    return jax.ShapeDtypeStruct(dims, dtype)


def pieces():
    return [(8 * zh + 2 * y, 8 * y + 2 * zh) for zh in range(4) for y in range(4)]


def rounded_dot(a, b, dims):
    return lax.dot_general(a, b, (dims, ((), ())), preferred_element_type=F32)


def image_kernel(far_logits, far_patches, far_cotangent, far_saved, send, dispatch, combine_term, *scratch):
    logits, patches, cotangent, saved, stage, arrived = scratch
    copies = [
        pltpu.make_async_copy(source, target, arrived.at[i])
        for i, (source, target) in enumerate(
            [
                (far_logits, logits),
                (far_patches, patches),
                (far_cotangent, cotangent),
                (far_saved, saved),
            ]
        )
    ]
    for copy in copies:
        copy.start()
    copies[0].wait()
    for new, old in pieces():
        dispatch[new : new + 2, :] = logits[0, old : old + 2, :]
    values = dispatch[...]
    top = jnp.exp(values - jnp.max(values, axis=1, keepdims=True))
    by_patch = top / jnp.sum(top, axis=1, keepdims=True)
    low = jnp.exp(values - jnp.max(values, axis=0, keepdims=True))
    by_slot = low / jnp.sum(low, axis=0, keepdims=True)
    dispatch[...] = by_patch
    copies[1].wait()
    slot_in = rounded_dot(by_patch.astype(BF16), patches[0], ((1,), (1,)))
    copies[2].wait()
    slot_grad = rounded_dot(by_slot.astype(BF16), cotangent[0], ((1,), (1,)))
    width = slot_in.shape[1]
    for zh in range(4):
        ins = slot_in[8 * zh : 8 * zh + 8, :].astype(BF16)
        grads = slot_grad[8 * zh : 8 * zh + 8, :].astype(BF16)
        for zl in range(4):
            send[4 * zh + zl, :, 0:width] = ins
            send[4 * zh + zl, :, width : 2 * width] = grads
    copies[3].wait()
    part = jnp.dot(saved[0], cotangent[0], preferred_element_type=F32)
    for new, old in pieces():
        stage[new : new + 2, :] = part[old : old + 2, :]
    part = stage[...]
    combine_term[...] = by_slot * (part - jnp.sum(by_slot * part, axis=0, keepdims=True))


def regroup_kernel(got, send, stage):
    width = got.shape[2] // 2
    for zh in range(4):
        for zl in range(4):
            block = got[4 * zh + zl].astype(F32)
            for kind in range(2):
                row = 32 * kind + 8 * zh
                stage[row : row + 8, width * zl : width * (zl + 1)] = block[
                    :, width * kind : width * (kind + 1)
                ]
    row = lax.broadcasted_iota(jnp.int32, (64, 64), 0)
    col = lax.broadcasted_iota(jnp.int32, (64, 64), 1)
    move = (row == (col % 8) * 8 + col // 8).astype(F32).astype(BF16)
    moved = jnp.dot(move, stage[...].astype(BF16), preferred_element_type=F32).astype(BF16)
    for x in range(4):
        send[8 * x : 8 * x + 8] = moved.reshape(8, 8, 4 * width)


GELU_SCALE = 0.7978845608028654
GELU_CUBE = 0.044715


def expert_kernel(rows, first, second, send, grad_before, after):
    both = rows[...].reshape(256, rows.shape[2])
    before = rounded_dot(both, first[0], ((1,), (1,)))
    grad_after = rounded_dot(both, second[0], ((1,), (1,)))
    grad_after = pltpu.roll(grad_after, 252, 0)
    is_in = lax.broadcasted_iota(jnp.int32, before.shape, 0) % 8 < 4
    square = before * before
    bent = jnp.tanh(GELU_SCALE * (before + GELU_CUBE * (before * square)))
    half = 0.5 * (1.0 + bent)
    slope = half + before * (
        (0.5 * GELU_SCALE) * ((1.0 - bent) * (1.0 + bent)) * (1.0 + (3.0 * GELU_CUBE) * square)
    )
    grads = jnp.where(is_in, grad_after * slope, 0.0)
    low = grads.astype(BF16)
    shifted = pltpu.roll(grads, 4, 0).astype(BF16)
    part = first.shape[2] // 2
    total = jnp.dot(low, first[0, :, :part], preferred_element_type=F32)
    total = total + jnp.dot(shifted, first[0, :, part:], preferred_element_type=F32)
    send[...] = total.astype(BF16).reshape(send.shape)
    grad_before[...] = low
    after[...] = pltpu.roll(jnp.where(is_in, before * half, 0.0), 4, 0).astype(BF16)


def weight_kernel(rows, grad_before, after, grad_first, grad_second):
    both = rows[...].reshape(256, rows.shape[2])
    grad_first[0] = rounded_dot(grad_before[...], both, ((0,), (0,))).astype(BF16)
    grad_second[0] = rounded_dot(after[...], both, ((0,), (0,))).astype(BF16)


def partial_kernel(got, send):
    total = got[0:8].astype(F32)
    for x in range(1, 4):
        total = total + got[8 * x : 8 * x + 8].astype(F32)
    low = total.reshape(64, got.shape[2]).astype(BF16)
    row = lax.broadcasted_iota(jnp.int32, (64, 64), 0)
    col = lax.broadcasted_iota(jnp.int32, (64, 64), 1)
    move = (row == (col % 8) * 8 + col // 8).astype(F32).astype(BF16)
    moved = jnp.dot(move, low, preferred_element_type=F32).astype(BF16)
    width = send.shape[2]
    for zh in range(4):
        for zl in range(4):
            at = (zl // 2) * 32 + 8 * zh
            lane = (zl % 2) * width
            send[4 * zh + zl] = moved[at : at + 8, lane : lane + width]


def back_kernel(got, patches, dispatch, combine_term, send, slot_back):
    for zh in range(4):
        total = got[4 * zh].astype(F32)
        for zl in range(1, 4):
            total = total + got[4 * zh + zl].astype(F32)
        slot_back[8 * zh : 8 * zh + 8, :] = total
    low = slot_back[...].astype(BF16)
    part = jnp.dot(low, patches[0], preferred_element_type=F32)
    by_patch = dispatch[...]
    grads = by_patch * (part - jnp.sum(by_patch * part, axis=1, keepdims=True))
    grads = (grads + combine_term[...]).astype(BF16)
    for zl in range(4):
        send[zl] = grads


def logit_kernel(got, patches, grad_logits, send, stage):
    total = got[0].astype(F32)
    for zl in range(1, 4):
        total = total + got[zl].astype(F32)
    low = total.astype(BF16)
    grad_logits[...] = low
    router = rounded_dot(low, patches[0], ((1,), (1,)))
    for new, old in pieces():
        stage[old : old + 2, :] = router[new : new + 2, :]
    router = stage[...].astype(BF16)
    for j in range(16):
        send[j] = router


def patch_kernel(dispatch, slot_back, grad_logits, router, grad_patches):
    new = lax.broadcasted_iota(jnp.int32, (32, 32), 0)
    old = lax.broadcasted_iota(jnp.int32, (32, 32), 1)
    move = (old == ((new // 2) % 4) * 8 + (new // 8) * 2 + new % 2).astype(F32).astype(BF16)
    columns = jnp.dot(move, router[...], preferred_element_type=F32)
    left = jnp.concatenate([dispatch[...], grad_logits[...].astype(F32)], axis=0).astype(BF16)
    right = jnp.concatenate([slot_back[...], columns], axis=0).astype(BF16)
    grad_patches[0] = rounded_dot(right, left, ((0,), (0,))).astype(BF16)


def add_kernel(got, send):
    total = got[0].astype(F32)
    for j in range(1, 16):
        total = total + got[j].astype(F32)
    low = total.astype(BF16)
    for j in range(8):
        send[j] = low


def total_kernel(got, grad_router):
    total = got[0].astype(F32)
    for j in range(1, 8):
        total = total + got[j].astype(F32)
    grad_router[...] = total


def exchange(value, axes):
    return lax.all_to_all(value, axes, 0, 0, tiled=True)


def body(patches, router, logits, slot_outputs, cotangent, weight_in, weight_out):
    count, width = patches.shape[1:]
    deep = weight_in.shape[1]
    hidden = weight_in.shape[2]
    patches = jnp.swapaxes(patches, 1, 2)
    cotangent = jnp.swapaxes(cotangent, 1, 2)
    send, dispatch, combine_term = pl.pallas_call(
        image_kernel,
        in_specs=[pl.BlockSpec(memory_space=pltpu.HBM)] * 4,
        scratch_shapes=[
            pltpu.VMEM(logits.shape, F32),
            pltpu.VMEM(patches.shape, BF16),
            pltpu.VMEM(cotangent.shape, BF16),
            pltpu.VMEM(slot_outputs.shape, BF16),
            pltpu.VMEM((32, count), F32),
            pltpu.SemaphoreType.DMA((4,)),
        ],
        compiler_params=pltpu.CompilerParams(vmem_limit_bytes=60 * 1024 * 1024),
        out_shape=[
            shape((16, 8, 2 * width), BF16),
            shape((32, count), F32),
            shape((32, count), F32),
        ],
    )(logits, patches, cotangent, slot_outputs)
    got = exchange(send, RING)
    send = call(
        regroup_kernel,
        shape((32, 8, deep), BF16),
        got,
        scratch=[pltpu.VMEM((64, deep), F32)],
    )
    rows = exchange(send, PLANE)
    send, grad_before, after = call(
        expert_kernel,
        [
            shape((32, 8, deep // 2), BF16),
            shape((256, hidden), BF16),
            shape((256, hidden), BF16),
        ],
        rows,
        jnp.swapaxes(weight_in, 1, 2),
        weight_out,
    )
    got = exchange(send, PLANE)
    grad_first, grad_second = call(
        weight_kernel,
        [shape((1, hidden, deep), BF16), shape((1, hidden, deep), BF16)],
        rows,
        grad_before,
        after,
    )
    send = call(partial_kernel, shape((16, 8, width), BF16), got)
    got = exchange(send, RING)
    send, slot_back = call(
        back_kernel,
        [shape((4, 32, count), BF16), shape((32, width), F32)],
        got,
        patches,
        dispatch,
        combine_term,
    )
    got = exchange(send, "tensor")
    grad_logits, send = call(
        logit_kernel,
        [shape((32, count), BF16), shape((16, 32, width), BF16)],
        got,
        patches,
        scratch=[pltpu.VMEM((32, width), F32)],
    )
    got = exchange(send, SHEET)
    grad_patches = call(
        patch_kernel,
        shape((1, width, count), BF16),
        dispatch,
        slot_back,
        grad_logits,
        jnp.swapaxes(router, 0, 1),
    )
    got = exchange(call(add_kernel, shape((8, 32, width), BF16), got), LINE)
    grad_router = call(total_kernel, shape((32, width), F32), got)
    return (
        jnp.swapaxes(grad_patches, 1, 2),
        jnp.swapaxes(grad_router, 0, 1),
        jnp.swapaxes(grad_first, 1, 2),
        grad_second,
    )


def solution(mesh):
    split = Mesh(mesh.devices.reshape(4, 4, 4, 2, 4), ("dp", "y", "zh", "core", "tensor"))
    images = ("dp", "y", "zh", "core")
    experts = ("y", "zh", "core")
    return jax.shard_map(
        body,
        mesh=split,
        in_specs=(
            P(images, None, "tensor"),
            P("tensor", None),
            P(images, None, None),
            P(images, None, "tensor"),
            P(images, None, "tensor"),
            P(experts, None, ("dp", "tensor")),
            P(experts, ("dp", "tensor"), None),
        ),
        out_specs=(
            P(images, None, "tensor"),
            P("tensor", None),
            P(experts, None, ("dp", "tensor")),
            P(experts, ("dp", "tensor"), None),
        ),
        check_vma=False,
    )
```

time: 144 us -> 135 us (0.938)
  the two profiles are of different devices: /device:TPU:1 before, /device:TPU:33 now
where the time goes in v2:
time: 135 us
  blocking collectives  99.7 us (74%)
  waiting for transfers between devices  16.2 us (12%)
  Pallas kernels  9.35 us (7%)
  starting transfers between devices  8.82 us (7%)
    all_to_all x6, blocking collectives, exchange(): return lax.all_to_all(value, axes, 0, 0, tiled=True)  99.7 us
    all_to_all x1, waiting for transfers between devices, exchange(): return lax.all_to_all(value, axes, 0, 0, tiled=True)  16.2 us
    all_to_all x1, starting transfers between devices, exchange(): return lax.all_to_all(value, axes, 0, 0, tiled=True)  8.82 us
    pallas_call x9, Pallas kernels, call(): pl.pallas_call(kernel, out_shape=outs, scratch_shapes=scratch, compiler_p...  6.7 us
  transfers between devices with their start and end apart: 1, of which 1 were waited for; matrix products, arithmetic and copies ran while one was open for 0% of the time, Pallas kernels for 2%

profile of v2, /device:TPU:33, one launch (start us, length us, event | category | flops | bytes accessed | tf_op | source)
XLA Modules:
  0.0 134.8 jit_solution(1352405940062892621)
XLA Ops:
  0.6 2.6 %shard_map.102 = (bf16[16,8,640]{2,1,0:T(8,128)(2,1)}, f32[32,576]{1,0:T(8,128)}, f32[32,576]{1,0:T(8,128)}) custom-call(f32[1,32,576]{2,1,0:T(8,128)} %far_logits.1, bf16[1,320,576]{2,1,0:T(8,128)(2,1)} %bitcast.7, bf16[1,320,576]{2,1,0:T(8,128)(2,1)} %bitcast.12, bf16[1,32,320]{2,1,0:T(8,128)(2,1)} %far_saved.1), custom_call_target="tpu_custom_call" | custom-call | tf_op jit(solution)/shard_map/pallas_call | solution.py:214
  3.3 28.5 %all_to_all.35.got = bf16[16,8,640]{2,1,0:T(8,128)(2,1)S(1)} all-to-all(bf16[16,8,640]{2,1,0:T(8,128)(2,1)} %get-tuple-element.17), channel_id=1, replica_groups=mesh['dp'=4,'y'=4,'zh'=4,'core'=2,'tensor'=4] {'zh','tensor'}, dimensions={0} | all-to-all | bytes 327680 | tf_op jit(solution)/shard_map/all_to_all | solution.py:205
  31.7 0.0 copy-start.2
  31.7 0.3 shard_map.103
  32.0 0.0 copy-start.1
  32.0 22.3 %all_to_all.36.rows = bf16[32,8,1280]{2,1,0:T(8,128)(2,1)S(1)} all-to-all(bf16[32,8,1280]{2,1,0:T(8,128)(2,1)S(1)} %shard_map.103), channel_id=1, replica_groups=mesh['dp'=4,'y'=4,'zh'=4,'core'=2,'tensor'=4] {'dp','y','core'}, dimensions={0} | all-to-all | bytes 1310720 | tf_op jit(solution)/shard_map/all_to_all | solution.py:205
  54.3 0.0 copy-done.2
  54.3 0.0 copy-done.1
  54.3 1.4 %shard_map.104 = (bf16[32,8,640]{2,1,0:T(8,128)(2,1)S(1)}, bf16[256,320]{1,0:T(8,128)(2,1)S(1)}, bf16[256,320]{1,0:T(8,128)(2,1)S(1)}) custom-call(bf16[32,8,1280]{2,1,0:T(8,128)(2,1)S(1)} %all_to_all.36.rows, bf16[1,320,1280]{2,1,0:T(8,128)(2,1)S(1)} %bitcast.10, bf16[1,320,1280]{2,1,0:T(8,128)(2,1)S(1)} %copy-done.2), custom_call_target="tpu_custom_call" | custom-call | tf_op jit(solution)/shard_map/pallas_call | solution.py:18
  55.7 13.2 %all_to_all.37.got = bf16[32,8,640]{2,1,0:T(8,128)(2,1)S(1)} all-to-all(bf16[32,8,640]{2,1,0:T(8,128)(2,1)S(1)} %get-tuple-element.18), channel_id=1, replica_groups=mesh['dp'=4,'y'=4,'zh'=4,'core'=2,'tensor'=4] {'dp','y','core'}, dimensions={0} | all-to-all | bytes 655360 | tf_op jit(solution)/shard_map/all_to_all | solution.py:205
  68.9 0.0 copy-start
  68.9 0.3 shard_map.105
  69.2 0.0 copy-start.3
  69.2 0.0 copy-start.4
  69.2 16.7 %all_to_all.38.got = bf16[16,8,320]{2,1,0:T(8,128)(2,1)S(1)} all-to-all(bf16[16,8,320]{2,1,0:T(8,128)(2,1)S(1)} %shard_map.105), channel_id=1, replica_groups=mesh['dp'=4,'y'=4,'zh'=4,'core'=2,'tensor'=4] {'zh','tensor'}, dimensions={0} | all-to-all | bytes 163840 | tf_op jit(solution)/shard_map/all_to_all | solution.py:205
  85.9 0.0 copy-done
  85.9 0.0 copy-done.3
  85.9 0.0 copy-done.4
  85.9 0.3 shard_map.106
  86.2 8.5 %all_to_all.39.got = bf16[4,32,576]{2,1,0:T(8,128)(2,1)S(1)} all-to-all(bf16[4,32,576]{2,1,0:T(8,128)(2,1)S(1)} %get-tuple-element.21), channel_id=1, replica_groups=mesh['dp'=4,'y'=4,'zh'=4,'core'=2,'tensor'=4] {'tensor'}, dimensions={0} | all-to-all | bytes 294912 | tf_op jit(solution)/shard_map/all_to_all | solution.py:205
  94.7 0.3 shard_map.107
  95.0 10.6 %all_to_all.40.got = bf16[16,32,320]{2,1,0:T(8,128)(2,1)S(1)} all-to-all(bf16[16,32,320]{2,1,0:T(8,128)(2,1)S(1)} %get-tuple-element.23), channel_id=1, replica_groups=mesh['dp'=4,'y'=4,'zh'=4,'core'=2,'tensor'=4] {'dp','y'}, dimensions={0} | all-to-all | bytes 655360 | tf_op jit(solution)/shard_map/all_to_all | solution.py:205
  105.6 0.7 shard_map.109
  106.4 8.8 %all-to-all-start.6 = ((bf16[8,32,320]{2,1,0:T(8,128)(2,1)}), bf16[8,32,320]{2,1,0:T(8,128)(2,1)S(1)}, u32[]{:S(2)}, u32[]{:S(2)}) async-start(bf16[8,32,320]{2,1,0:T(8,128)(2,1)} %shard_map.109), calls=%async_computation.6 | async-start | bytes 393216 | tf_op jit(solution)/shard_map/all_to_all | solution.py:205
  115.2 0.0 copy-start.5
  115.2 1.6 %shard_map.111 = (bf16[1,320,1280]{2,1,0:T(8,128)(2,1)}, bf16[1,320,1280]{2,1,0:T(8,128)(2,1)}) custom-call(bf16[32,8,1280]{2,1,0:T(8,128)(2,1)S(1)} %all_to_all.36.rows, bf16[256,320]{1,0:T(8,128)(2,1)S(1)} %get-tuple-element.24.grad_before, bf16[256,320]{1,0:T(8,128)(2,1)S(1)} %get-tuple-element.25.after), custom_call_target="tpu_custom_call" | custom-call | tf_op jit(solution)/shard_map/pallas_call | solution.py:18
  116.8 0.0 copy-done.5
  116.8 1.2 shard_map.108
  118.0 16.2 %all-to-all-done.6.got = bf16[8,32,320]{2,1,0:T(8,128)(2,1)S(1)} async-done(((bf16[8,32,320]{2,1,0:T(8,128)(2,1)}), bf16[8,32,320]{2,1,0:T(8,128)(2,1)S(1)}, u32[]{:S(2)}, u32[]{:S(2)}) %all-to-all-start.6) | async-done | bytes 163872 | tf_op jit(solution)/shard_map/all_to_all | solution.py:205
  134.2 0.6 shard_map.110
Async XLA Ops:
  31.7 22.6 %copy-start.2 = (bf16[1,320,1280]{2,1,0:T(8,128)(2,1)S(1)}, bf16[1,320,1280]{2,1,0:T(8,128)(2,1)}, u32[]{:S(2)}) copy-start(bf16[1,320,1280]{2,1,0:T(8,128)(2,1)} %second.1) | copy-start | bytes 2457604
  32.0 22.3 %copy-start.1 = (bf16[1,1280,320]{1,2,0:T(8,128)(2,1)S(1)}, bf16[1,1280,320]{1,2,0:T(8,128)(2,1)}, u32[]{:S(2)}) copy-start(bf16[1,1280,320]{1,2,0:T(8,128)(2,1)} %param.12) | copy-start | bytes 2457604
  68.9 17.0 %copy-start = (bf16[1,576,320]{1,2,0:T(8,128)(2,1)S(1)}, bf16[1,576,320]{1,2,0:T(8,128)(2,1)}, u32[]{:S(2)}) copy-start(bf16[1,576,320]{1,2,0:T(8,128)(2,1)} %param.7) | copy-start | bytes 1105924
  69.2 16.7 %copy-start.3 = (f32[32,576]{1,0:T(8,128)S(1)}, f32[32,576]{1,0:T(8,128)}, u32[]{:S(2)}) copy-start(f32[32,576]{1,0:T(8,128)} %get-tuple-element.16.dispatch) | copy-start | bytes 221188
  69.2 16.7 %copy-start.4 = (f32[32,576]{1,0:T(8,128)S(1)}, f32[32,576]{1,0:T(8,128)}, u32[]{:S(2)}) copy-start(f32[32,576]{1,0:T(8,128)} %get-tuple-element.19.combine_term) | copy-start | bytes 221188
  106.4 27.8 %all-to-all-start.6 = ((bf16[8,32,320]{2,1,0:T(8,128)(2,1)}), bf16[8,32,320]{2,1,0:T(8,128)(2,1)S(1)}, u32[]{:S(2)}, u32[]{:S(2)}) async-start(bf16[8,32,320]{2,1,0:T(8,128)(2,1)} %shard_map.109), calls=%async_computation.6 | async-start | bytes 393216 | tf_op jit(solution)/shard_map/all_to_all | solution.py:205
  115.2 1.6 %copy-start.5 = (bf16[320,32]{0,1:T(8,128)(2,1)S(1)}, bf16[320,32]{0,1:T(8,128)(2,1)}, u32[]{:S(2)}) copy-start(bf16[320,32]{0,1:T(8,128)(2,1)} %param.8) | copy-start | bytes 61444

commit v3 on v2

--- a/solution.py
+++ b/solution.py
@@ -10,8 +10,6 @@
 BF16 = jnp.bfloat16
 RING = ("zh", "tensor")
 PLANE = ("dp", "y", "core")
-SHEET = ("dp", "y")
-LINE = ("zh", "core")
 
 
 def call(kernel, outs, *args, scratch=()):
@@ -35,17 +33,17 @@
     return lax.dot_general(a, b, (dims, ((), ())), preferred_element_type=F32)
 
 
-def image_kernel(far_logits, far_patches, far_cotangent, far_saved, send, dispatch, combine_term, *scratch):
-    logits, patches, cotangent, saved, stage, arrived = scratch
+def soft(values, axis):
+    top = jnp.exp(values - jnp.max(values, axis=axis, keepdims=True))
+    return top / jnp.sum(top, axis=axis, keepdims=True)
+
+
+def image_kernel(far_logits, far_patches, far_cotangent, send, dispatch, *scratch):
+    logits, patches, cotangent, arrived = scratch
     copies = [
         pltpu.make_async_copy(source, target, arrived.at[i])
         for i, (source, target) in enumerate(
-            [
-                (far_logits, logits),
-                (far_patches, patches),
-                (far_cotangent, cotangent),
-                (far_saved, saved),
-            ]
+            [(far_logits, logits), (far_patches, patches), (far_cotangent, cotangent)]
         )
     ]
     for copy in copies:
@@ -54,10 +52,8 @@
     for new, old in pieces():
         dispatch[new : new + 2, :] = logits[0, old : old + 2, :]
     values = dispatch[...]
-    top = jnp.exp(values - jnp.max(values, axis=1, keepdims=True))
-    by_patch = top / jnp.sum(top, axis=1, keepdims=True)
-    low = jnp.exp(values - jnp.max(values, axis=0, keepdims=True))
-    by_slot = low / jnp.sum(low, axis=0, keepdims=True)
+    by_patch = soft(values, 1)
+    by_slot = soft(values, 0)
     dispatch[...] = by_patch
     copies[1].wait()
     slot_in = rounded_dot(by_patch.astype(BF16), patches[0], ((1,), (1,)))
@@ -70,12 +66,14 @@
         for zl in range(4):
             send[4 * zh + zl, :, 0:width] = ins
             send[4 * zh + zl, :, width : 2 * width] = grads
-    copies[3].wait()
+
+
+def combine_kernel(logits, cotangent, saved, combine_term):
+    by_slot = soft(logits[0], 0)
     part = jnp.dot(saved[0], cotangent[0], preferred_element_type=F32)
+    term = by_slot * (part - jnp.sum(by_slot * part, axis=0, keepdims=True))
     for new, old in pieces():
-        stage[new : new + 2, :] = part[old : old + 2, :]
-    part = stage[...]
-    combine_term[...] = by_slot * (part - jnp.sum(by_slot * part, axis=0, keepdims=True))
+        combine_term[new : new + 2, :] = term[old : old + 2, :]
 
 
 def regroup_kernel(got, send, stage):
@@ -170,9 +168,15 @@
     router = rounded_dot(low, patches[0], ((1,), (1,)))
     for new, old in pieces():
         stage[old : old + 2, :] = router[new : new + 2, :]
-    router = stage[...].astype(BF16)
-    for j in range(16):
-        send[j] = router
+    for core in range(2):
+        at = 16 * core
+        rows = stage[at : at + 16, :].astype(BF16)
+        rest = jnp.concatenate([stage[at : at + 8, 256:], stage[at + 8 : at + 16, 256:]], axis=1)
+        rest = rest.astype(BF16)
+        for j in range(16):
+            send[2 * j + core, 0:16, :] = rows[:, 0:128]
+            send[2 * j + core, 16:32, :] = rows[:, 128:256]
+            send[2 * j + core, 32:40, :] = rest
 
 
 def patch_kernel(dispatch, slot_back, grad_logits, router, grad_patches):
@@ -187,18 +191,23 @@
 
 def add_kernel(got, send):
     total = got[0].astype(F32)
-    for j in range(1, 16):
+    for j in range(1, got.shape[0]):
         total = total + got[j].astype(F32)
-    low = total.astype(BF16)
-    for j in range(8):
-        send[j] = low
+    total = total.astype(send.dtype)
+    for j in range(send.shape[0]):
+        send[j] = total
 
 
 def total_kernel(got, grad_router):
-    total = got[0].astype(F32)
-    for j in range(1, 8):
-        total = total + got[j].astype(F32)
-    grad_router[...] = total
+    for core in range(2):
+        at = 16 * core
+        total = got[core].astype(F32)
+        for zh in range(1, 4):
+            total = total + got[2 * zh + core].astype(F32)
+        grad_router[at : at + 16, 0:128] = total[0:16, :]
+        grad_router[at : at + 16, 128:256] = total[16:32, :]
+        grad_router[at : at + 8, 256:320] = total[32:40, 0:64]
+        grad_router[at + 8 : at + 16, 256:320] = total[32:40, 64:128]
 
 
 def exchange(value, axes):
@@ -211,25 +220,25 @@
     hidden = weight_in.shape[2]
     patches = jnp.swapaxes(patches, 1, 2)
     cotangent = jnp.swapaxes(cotangent, 1, 2)
-    send, dispatch, combine_term = pl.pallas_call(
+    send, dispatch = pl.pallas_call(
         image_kernel,
-        in_specs=[pl.BlockSpec(memory_space=pltpu.HBM)] * 4,
+        in_specs=[pl.BlockSpec(memory_space=pltpu.HBM)] * 3,
         scratch_shapes=[
             pltpu.VMEM(logits.shape, F32),
             pltpu.VMEM(patches.shape, BF16),
             pltpu.VMEM(cotangent.shape, BF16),
-            pltpu.VMEM(slot_outputs.shape, BF16),
-            pltpu.VMEM((32, count), F32),
-            pltpu.SemaphoreType.DMA((4,)),
+            pltpu.SemaphoreType.DMA((3,)),
         ],
         compiler_params=pltpu.CompilerParams(vmem_limit_bytes=60 * 1024 * 1024),
         out_shape=[
             shape((16, 8, 2 * width), BF16),
             shape((32, count), F32),
-            shape((32, count), F32),
         ],
-    )(logits, patches, cotangent, slot_outputs)
-    got = exchange(send, RING)
+    )(logits, patches, cotangent)
+    combine_term = call(
+        combine_kernel, shape((32, count), F32), logits, cotangent, slot_outputs
+    )
+    got, combine_term = lax.optimization_barrier((exchange(send, RING), combine_term))
     send = call(
         regroup_kernel,
         shape((32, 8, deep), BF16),
@@ -269,12 +278,12 @@
     got = exchange(send, "tensor")
     grad_logits, send = call(
         logit_kernel,
-        [shape((32, count), BF16), shape((16, 32, width), BF16)],
+        [shape((32, count), BF16), shape((32, 40, 128), BF16)],
         got,
         patches,
         scratch=[pltpu.VMEM((32, width), F32)],
     )
-    got = exchange(send, SHEET)
+    got = exchange(send, PLANE)
     grad_patches = call(
         patch_kernel,
         shape((1, width, count), BF16),
@@ -283,7 +292,7 @@
         grad_logits,
         jnp.swapaxes(router, 0, 1),
     )
-    got = exchange(call(add_kernel, shape((8, 32, width), BF16), got), LINE)
+    got = exchange(call(add_kernel, shape((8, 40, 128), BF16), got), ("zh", "core"))
     grad_router = call(total_kernel, shape((32, width), F32), got)
     return (
         jnp.swapaxes(grad_patches, 1, 2),

time: 135 us -> 131 us (0.970)
  the two profiles are of different devices: /device:TPU:33 before, /device:TPU:1 now
where the time goes in v3:
time: 131 us
  blocking collectives  78.3 us (60%)
  waiting for transfers between devices  21.5 us (16%)
  starting transfers between devices  20.8 us (16%)
  Pallas kernels  9.48 us (7%)
    all_to_all x5, blocking collectives, exchange(): return lax.all_to_all(value, axes, 0, 0, tiled=True)  78.3 us
    all_to_all x2, waiting for transfers between devices, exchange(): return lax.all_to_all(value, axes, 0, 0, tiled=True)  21.5 us
    all_to_all x2, starting transfers between devices, exchange(): return lax.all_to_all(value, axes, 0, 0, tiled=True)  20.8 us
    pallas_call x10, Pallas kernels, call(): pl.pallas_call(kernel, out_shape=outs, scratch_shapes=scratch, compiler_p...  6.97 us
  transfers between devices with their start and end apart: 2, of which 2 were waited for; matrix products, arithmetic and copies ran while one was open for 0% of the time, Pallas kernels for 2%

profile of v3, /device:TPU:1, one launch (start us, length us, event | category | flops | bytes accessed | tf_op | source)
XLA Modules:
  0.0 130.9 jit_solution(5017591509605755756)
XLA Ops:
  0.6 0.0 copy-start.1
  0.6 2.5 %shard_map.102 = (bf16[16,8,640]{2,1,0:T(8,128)(2,1)}, f32[32,576]{1,0:T(8,128)}) custom-call(f32[1,32,576]{2,1,0:T(8,128)} %logits.1, bf16[1,320,576]{2,1,0:T(8,128)(2,1)} %bitcast.7, bf16[1,320,576]{2,1,0:T(8,128)(2,1)} %bitcast.10), custom_call_target="tpu_custom_call" | custom-call | tf_op jit(solution)/shard_map/pallas_call | solution.py:223
  3.2 0.0 copy-start.4
  3.2 0.0 copy-start.6
  3.2 15.9 %all-to-all-start = ((bf16[16,8,640]{2,1,0:T(8,128)(2,1)}), bf16[16,8,640]{2,1,0:T(8,128)(2,1)S(1)}, u32[]{:S(2)}, u32[]{:S(2)}) async-start(bf16[16,8,640]{2,1,0:T(8,128)(2,1)} %get-tuple-element.18), calls=%async_computation | async-start | bytes 327680 | tf_op jit(solution)/shard_map/all_to_all | solution.py:214
  19.1 0.0 copy-done.1
  19.1 0.0 copy-done.4
  19.1 0.0 copy-done.6
  19.1 0.2 shard_map.103.combine_term
  19.3 12.0 %all-to-all-done.got = bf16[16,8,640]{2,1,0:T(8,128)(2,1)S(1)} async-done(((bf16[16,8,640]{2,1,0:T(8,128)(2,1)}), bf16[16,8,640]{2,1,0:T(8,128)(2,1)S(1)}, u32[]{:S(2)}, u32[]{:S(2)}) %all-to-all-start) | async-done | bytes 163872 | tf_op jit(solution)/shard_map/all_to_all | solution.py:214
  31.3 0.3 shard_map.104
  31.6 0.0 copy-start.2
  31.6 24.3 %all_to_all.35.rows = bf16[32,8,1280]{2,1,0:T(8,128)(2,1)S(1)} all-to-all(bf16[32,8,1280]{2,1,0:T(8,128)(2,1)S(1)} %shard_map.104), channel_id=1, replica_groups=mesh['dp'=4,'y'=4,'zh'=4,'core'=2,'tensor'=4] {'dp','y','core'}, dimensions={0} | all-to-all | bytes 1310720 | tf_op jit(solution)/shard_map/all_to_all | solution.py:214
  55.9 0.0 copy-done.3
  55.9 0.0 copy-done.2
  55.9 1.4 %shard_map.105 = (bf16[32,8,640]{2,1,0:T(8,128)(2,1)S(1)}, bf16[256,320]{1,0:T(8,128)(2,1)S(1)}, bf16[256,320]{1,0:T(8,128)(2,1)S(1)}) custom-call(bf16[32,8,1280]{2,1,0:T(8,128)(2,1)S(1)} %all_to_all.35.rows, bf16[1,320,1280]{2,1,0:T(8,128)(2,1)S(1)} %bitcast.12, bf16[1,320,1280]{2,1,0:T(8,128)(2,1)S(1)} %copy-done.3), custom_call_target="tpu_custom_call" | custom-call | tf_op jit(solution)/shard_map/pallas_call | solution.py:16
  57.4 13.2 %all_to_all.36.got = bf16[32,8,640]{2,1,0:T(8,128)(2,1)S(1)} all-to-all(bf16[32,8,640]{2,1,0:T(8,128)(2,1)S(1)} %get-tuple-element.20), channel_id=1, replica_groups=mesh['dp'=4,'y'=4,'zh'=4,'core'=2,'tensor'=4] {'dp','y','core'}, dimensions={0} | all-to-all | bytes 655360 | tf_op jit(solution)/shard_map/all_to_all | solution.py:214
  70.5 0.3 shard_map.106
  70.8 0.0 copy-start.5
  70.8 15.9 %all_to_all.37.got = bf16[16,8,320]{2,1,0:T(8,128)(2,1)S(1)} all-to-all(bf16[16,8,320]{2,1,0:T(8,128)(2,1)S(1)} %shard_map.106), channel_id=1, replica_groups=mesh['dp'=4,'y'=4,'zh'=4,'core'=2,'tensor'=4] {'zh','tensor'}, dimensions={0} | all-to-all | bytes 163840 | tf_op jit(solution)/shard_map/all_to_all | solution.py:214
  86.7 0.0 copy-done
  86.7 0.0 copy-done.5
  86.7 0.3 shard_map.107
  87.0 9.8 %all_to_all.38.got = bf16[4,32,576]{2,1,0:T(8,128)(2,1)S(1)} all-to-all(bf16[4,32,576]{2,1,0:T(8,128)(2,1)S(1)} %get-tuple-element.23), channel_id=1, replica_groups=mesh['dp'=4,'y'=4,'zh'=4,'core'=2,'tensor'=4] {'tensor'}, dimensions={0} | all-to-all | bytes 294912 | tf_op jit(solution)/shard_map/all_to_all | solution.py:214
  96.8 0.3 shard_map.108
  97.1 15.1 %all_to_all.39.got = bf16[32,40,128]{2,1,0:T(8,128)(2,1)S(1)} all-to-all(bf16[32,40,128]{2,1,0:T(8,128)(2,1)S(1)} %get-tuple-element.25), channel_id=1, replica_groups=mesh['dp'=4,'y'=4,'zh'=4,'core'=2,'tensor'=4] {'dp','y','core'}, dimensions={0} | all-to-all | bytes 655360 | tf_op jit(solution)/shard_map/all_to_all | solution.py:214
  112.2 0.7 shard_map.110
  113.0 5.0 %all-to-all-start.6 = ((bf16[8,40,128]{2,1,0:T(8,128)(2,1)}), bf16[8,40,128]{2,1,0:T(8,128)(2,1)S(1)}, u32[]{:S(2)}, u32[]{:S(2)}) async-start(bf16[8,40,128]{2,1,0:T(8,128)(2,1)} %shard_map.110), calls=%async_computation.6 | async-start | bytes 163840 | tf_op jit(solution)/shard_map/all_to_all | solution.py:214
  117.9 1.6 %shard_map.112 = (bf16[1,320,1280]{2,1,0:T(8,128)(2,1)}, bf16[1,320,1280]{2,1,0:T(8,128)(2,1)}) custom-call(bf16[32,8,1280]{2,1,0:T(8,128)(2,1)S(1)} %all_to_all.35.rows, bf16[256,320]{1,0:T(8,128)(2,1)S(1)} %get-tuple-element.26.grad_before, bf16[256,320]{1,0:T(8,128)(2,1)S(1)} %get-tuple-element.27.after), custom_call_target="tpu_custom_call" | custom-call | tf_op jit(solution)/shard_map/pallas_call | solution.py:16
  119.5 1.2 shard_map.109
  120.7 9.5 %all-to-all-done.6.got = bf16[8,40,128]{2,1,0:T(8,128)(2,1)S(1)} async-done(((bf16[8,40,128]{2,1,0:T(8,128)(2,1)}), bf16[8,40,128]{2,1,0:T(8,128)(2,1)S(1)}, u32[]{:S(2)}, u32[]{:S(2)}) %all-to-all-start.6) | async-done | bytes 81952 | tf_op jit(solution)/shard_map/all_to_all | solution.py:214
  130.2 0.7 shard_map.111
  (4 shorter events, 0.0 us)
Async XLA Ops:
  0.6 18.4 %copy-start.1 = (bf16[1,576,320]{1,2,0:T(8,128)(2,1)S(1)}, bf16[1,576,320]{1,2,0:T(8,128)(2,1)}, u32[]{:S(2)}) copy-start(bf16[1,576,320]{1,2,0:T(8,128)(2,1)} %param.11) | copy-start | bytes 1105924
  3.2 15.9 %copy-start.4 = (f32[1,32,576]{2,1,0:T(8,128)S(1)}, f32[1,32,576]{2,1,0:T(8,128)}, u32[]{:S(2)}) copy-start(f32[1,32,576]{2,1,0:T(8,128)} %logits.1) | copy-start | bytes 221188
  3.2 15.9 %copy-start.6 = (bf16[1,32,320]{2,1,0:T(8,128)(2,1)S(1)}, bf16[1,32,320]{2,1,0:T(8,128)(2,1)}, u32[]{:S(2)}) copy-start(bf16[1,32,320]{2,1,0:T(8,128)(2,1)} %saved.1) | copy-start | bytes 61444
  3.2 28.1 %all-to-all-start = ((bf16[16,8,640]{2,1,0:T(8,128)(2,1)}), bf16[16,8,640]{2,1,0:T(8,128)(2,1)S(1)}, u32[]{:S(2)}, u32[]{:S(2)}) async-start(bf16[16,8,640]{2,1,0:T(8,128)(2,1)} %get-tuple-element.18), calls=%async_computation | async-start | bytes 327680 | tf_op jit(solution)/shard_map/all_to_all | solution.py:214
  31.3 24.6 %copy-start.3 = (bf16[1,320,1280]{2,1,0:T(8,128)(2,1)S(1)}, bf16[1,320,1280]{2,1,0:T(8,128)(2,1)}, u32[]{:S(2)}) copy-start(bf16[1,320,1280]{2,1,0:T(8,128)(2,1)} %second.1) | copy-start | bytes 2457604
  31.6 24.3 %copy-start.2 = (bf16[1,1280,320]{1,2,0:T(8,128)(2,1)S(1)}, bf16[1,1280,320]{1,2,0:T(8,128)(2,1)}, u32[]{:S(2)}) copy-start(bf16[1,1280,320]{1,2,0:T(8,128)(2,1)} %param.12) | copy-start | bytes 2457604
  70.5 16.2 %copy-start = (bf16[1,576,320]{1,2,0:T(8,128)(2,1)S(1)}, bf16[1,576,320]{1,2,0:T(8,128)(2,1)}, u32[]{:S(2)}) copy-start(bf16[1,576,320]{1,2,0:T(8,128)(2,1)} %param.7) | copy-start | bytes 1105924
  70.8 15.9 %copy-start.5 = (f32[32,576]{1,0:T(8,128)S(1)}, f32[32,576]{1,0:T(8,128)}, u32[]{:S(2)}) copy-start(f32[32,576]{1,0:T(8,128)} %get-tuple-element.17.dispatch) | copy-start | bytes 221188
  113.0 17.2 %all-to-all-start.6 = ((bf16[8,40,128]{2,1,0:T(8,128)(2,1)}), bf16[8,40,128]{2,1,0:T(8,128)(2,1)S(1)}, u32[]{:S(2)}, u32[]{:S(2)}) async-start(bf16[8,40,128]{2,1,0:T(8,128)(2,1)} %shard_map.110), calls=%async_computation.6 | async-start | bytes 163840 | tf_op jit(solution)/shard_map/all_to_all | solution.py:214
  117.9 1.6 %copy-start.7 = (bf16[320,32]{0,1:T(8,128)(2,1)S(1)}, bf16[320,32]{0,1:T(8,128)(2,1)}, u32[]{:S(2)}) copy-start(bf16[320,32]{0,1:T(8,128)(2,1)} %param.8) | copy-start | bytes 61444

commit v4 on v3

--- a/solution.py
+++ b/solution.py
@@ -68,14 +68,6 @@
             send[4 * zh + zl, :, width : 2 * width] = grads
 
 
-def combine_kernel(logits, cotangent, saved, combine_term):
-    by_slot = soft(logits[0], 0)
-    part = jnp.dot(saved[0], cotangent[0], preferred_element_type=F32)
-    term = by_slot * (part - jnp.sum(by_slot * part, axis=0, keepdims=True))
-    for new, old in pieces():
-        combine_term[new : new + 2, :] = term[old : old + 2, :]
-
-
 def regroup_kernel(got, send, stage):
     width = got.shape[2] // 2
     for zh in range(4):
@@ -98,7 +90,14 @@
 GELU_CUBE = 0.044715
 
 
-def expert_kernel(rows, first, second, send, grad_before, after):
+def expert_kernel(
+    rows, first, second, logits, cotangent, saved, send, grad_before, after, combine_term
+):
+    by_slot = soft(logits[0], 0)
+    part = jnp.dot(saved[0], cotangent[0], preferred_element_type=F32)
+    term = by_slot * (part - jnp.sum(by_slot * part, axis=0, keepdims=True))
+    for new, old in pieces():
+        combine_term[new : new + 2, :] = term[old : old + 2, :]
     both = rows[...].reshape(256, rows.shape[2])
     before = rounded_dot(both, first[0], ((1,), (1,)))
     grad_after = rounded_dot(both, second[0], ((1,), (1,)))
@@ -229,16 +228,13 @@
             pltpu.VMEM(cotangent.shape, BF16),
             pltpu.SemaphoreType.DMA((3,)),
         ],
-        compiler_params=pltpu.CompilerParams(vmem_limit_bytes=60 * 1024 * 1024),
+        compiler_params=pltpu.CompilerParams(vmem_limit_bytes=24 * 1024 * 1024),
         out_shape=[
             shape((16, 8, 2 * width), BF16),
             shape((32, count), F32),
         ],
-    )(logits, patches, cotangent)
-    combine_term = call(
-        combine_kernel, shape((32, count), F32), logits, cotangent, slot_outputs
-    )
-    got, combine_term = lax.optimization_barrier((exchange(send, RING), combine_term))
+    )(*[pltpu.with_memory_space_constraint(a, pltpu.HBM) for a in (logits, patches, cotangent)])
+    got = exchange(send, RING)
     send = call(
         regroup_kernel,
         shape((32, 8, deep), BF16),
@@ -246,16 +242,20 @@
         scratch=[pltpu.VMEM((64, deep), F32)],
     )
     rows = exchange(send, PLANE)
-    send, grad_before, after = call(
+    send, grad_before, after, combine_term = call(
         expert_kernel,
         [
             shape((32, 8, deep // 2), BF16),
             shape((256, hidden), BF16),
             shape((256, hidden), BF16),
+            shape((32, count), F32),
         ],
         rows,
         jnp.swapaxes(weight_in, 1, 2),
         weight_out,
+        logits,
+        cotangent,
+        slot_outputs,
     )
     got = exchange(send, PLANE)
     grad_first, grad_second = call(

time: 131 us -> 130 us (level)
  blocking collectives: 78.3 us -> 106 us
  starting transfers between devices: 20.8 us -> 4.96 us
  waiting for transfers between devices: 21.5 us -> 9.48 us
    all_to_all x5 -> x6, blocking collectives: 78.3 us -> 106 us  [exchange(): return lax.all_to_all(value, axes, 0, 0, tiled=True)]
    all_to_all x2 -> x1, starting transfers between devices: 20.8 us -> 4.96 us  [exchange(): return lax.all_to_all(value, axes, 0, 0, tiled=True)]
    all_to_all x2 -> x1, waiting for transfers between devices: 21.5 us -> 9.48 us  [exchange(): return lax.all_to_all(value, axes, 0, 0, tiled=True)]
    pallas_call x10 -> x9, Pallas kernels: 6.97 us -> 6.82 us  [call(): pl.pallas_call(kernel, out_shape=outs, scratch_shapes=scratch, compiler_p...]
  transfers between devices with their start and end apart: 2 -> 1, of which waited for: 2 -> 1; matrix products, arithmetic and copies ran while one was open for 0% -> 0% of each run, Pallas kernels for 2% -> 2%
where the time goes in v4:
time: 130 us
  blocking collectives  106 us (82%)
  waiting for transfers between devices  9.48 us (7%)
  Pallas kernels  8.61 us (7%)
  starting transfers between devices  4.96 us (4%)
    all_to_all x6, blocking collectives, exchange(): return lax.all_to_all(value, axes, 0, 0, tiled=True)  106 us
    all_to_all x1, waiting for transfers between devices, exchange(): return lax.all_to_all(value, axes, 0, 0, tiled=True)  9.48 us
    pallas_call x9, Pallas kernels, call(): pl.pallas_call(kernel, out_shape=outs, scratch_shapes=scratch, compiler_p...  6.82 us
    all_to_all x1, starting transfers between devices, exchange(): return lax.all_to_all(value, axes, 0, 0, tiled=True)  4.96 us
  transfers between devices with their start and end apart: 1, of which 1 were waited for; matrix products, arithmetic and copies ran while one was open for 0% of the time, Pallas kernels for 2%

profile of v4, /device:TPU:1, one launch (start us, length us, event | category | flops | bytes accessed | tf_op | source)
XLA Modules:
  0.0 129.7 jit_solution(18007343123351563930)
XLA Ops:
  0.6 1.8 %shard_map.102 = (bf16[16,8,640]{2,1,0:T(8,128)(2,1)S(1)}, f32[32,576]{1,0:T(8,128)S(1)}) custom-call(f32[1,32,576]{2,1,0:T(8,128)} %logits.1, bf16[1,320,576]{2,1,0:T(8,128)(2,1)} %bitcast.7, bf16[1,320,576]{2,1,0:T(8,128)(2,1)} %bitcast.10), custom_call_target="tpu_custom_call" | custom-call | tf_op jit(solution)/shard_map/pallas_call | solution.py:222
  2.4 0.0 copy-start.5
  2.4 27.8 %all_to_all.35.got = bf16[16,8,640]{2,1,0:T(8,128)(2,1)S(1)} all-to-all(bf16[16,8,640]{2,1,0:T(8,128)(2,1)S(1)} %get-tuple-element.17), channel_id=1, replica_groups=mesh['dp'=4,'y'=4,'zh'=4,'core'=2,'tensor'=4] {'zh','tensor'}, dimensions={0} | all-to-all | bytes 327680 | tf_op jit(solution)/shard_map/all_to_all | solution.py:213
  30.2 0.0 copy-start.3
  30.2 0.3 shard_map.103
  30.5 0.0 copy-start.1
  30.5 0.0 copy-start.2
  30.5 0.0 copy-start.4
  30.5 24.3 %all_to_all.36.rows = bf16[32,8,1280]{2,1,0:T(8,128)(2,1)S(1)} all-to-all(bf16[32,8,1280]{2,1,0:T(8,128)(2,1)S(1)} %shard_map.103), channel_id=1, replica_groups=mesh['dp'=4,'y'=4,'zh'=4,'core'=2,'tensor'=4] {'dp','y','core'}, dimensions={0} | all-to-all | bytes 1310720 | tf_op jit(solution)/shard_map/all_to_all | solution.py:213
  54.8 0.0 copy-done.5
  54.8 0.0 copy-done.3
  54.8 0.0 copy-done.1
  54.8 0.0 copy-done.2
  54.9 0.0 copy-done.4
  54.9 1.5 %shard_map.104 = (bf16[32,8,640]{2,1,0:T(8,128)(2,1)S(1)}, bf16[256,320]{1,0:T(8,128)(2,1)S(1)}, bf16[256,320]{1,0:T(8,128)(2,1)S(1)}, f32[32,576]{1,0:T(8,128)S(1)}) custom-call(bf16[32,8,1280]{2,1,0:T(8,128)(2,1)S(1)} %all_to_all.36.rows, bf16[1,320,1280]{2,1,0:T(8,128)(2,1)S(1)} %bitcast.12, bf16[1,320,1280]{2,1,0:T(8,128)(2,1)S(1)} %copy-done.3, ...), custom_call_target="tpu_custom_call" | custom-call | tf_op jit(solution)/shard_map/pallas_call | solution.py:16
  56.4 13.2 %all_to_all.37.got = bf16[32,8,640]{2,1,0:T(8,128)(2,1)S(1)} all-to-all(bf16[32,8,640]{2,1,0:T(8,128)(2,1)S(1)} %get-tuple-element.18), channel_id=1, replica_groups=mesh['dp'=4,'y'=4,'zh'=4,'core'=2,'tensor'=4] {'dp','y','core'}, dimensions={0} | all-to-all | bytes 655360 | tf_op jit(solution)/shard_map/all_to_all | solution.py:213
  69.5 0.0 copy-start
  69.5 0.3 shard_map.105
  69.8 15.7 %all_to_all.38.got = bf16[16,8,320]{2,1,0:T(8,128)(2,1)S(1)} all-to-all(bf16[16,8,320]{2,1,0:T(8,128)(2,1)S(1)} %shard_map.105), channel_id=1, replica_groups=mesh['dp'=4,'y'=4,'zh'=4,'core'=2,'tensor'=4] {'zh','tensor'}, dimensions={0} | all-to-all | bytes 163840 | tf_op jit(solution)/shard_map/all_to_all | solution.py:213
  85.6 0.0 copy-done
  85.6 0.3 shard_map.106
  85.8 9.8 %all_to_all.39.got = bf16[4,32,576]{2,1,0:T(8,128)(2,1)S(1)} all-to-all(bf16[4,32,576]{2,1,0:T(8,128)(2,1)S(1)} %get-tuple-element.21), channel_id=1, replica_groups=mesh['dp'=4,'y'=4,'zh'=4,'core'=2,'tensor'=4] {'tensor'}, dimensions={0} | all-to-all | bytes 294912 | tf_op jit(solution)/shard_map/all_to_all | solution.py:213
  95.6 0.3 shard_map.107
  96.0 15.2 %all_to_all.40.got = bf16[32,40,128]{2,1,0:T(8,128)(2,1)S(1)} all-to-all(bf16[32,40,128]{2,1,0:T(8,128)(2,1)S(1)} %get-tuple-element.23), channel_id=1, replica_groups=mesh['dp'=4,'y'=4,'zh'=4,'core'=2,'tensor'=4] {'dp','y','core'}, dimensions={0} | all-to-all | bytes 655360 | tf_op jit(solution)/shard_map/all_to_all | solution.py:213
  111.1 0.7 shard_map.109
  111.8 5.0 %all-to-all-start.6 = ((bf16[8,40,128]{2,1,0:T(8,128)(2,1)}), bf16[8,40,128]{2,1,0:T(8,128)(2,1)S(1)}, u32[]{:S(2)}, u32[]{:S(2)}) async-start(bf16[8,40,128]{2,1,0:T(8,128)(2,1)} %shard_map.109), calls=%async_computation.6 | async-start | bytes 163840 | tf_op jit(solution)/shard_map/all_to_all | solution.py:213
  116.8 0.0 copy-start.6
  116.8 1.6 %shard_map.111 = (bf16[1,320,1280]{2,1,0:T(8,128)(2,1)}, bf16[1,320,1280]{2,1,0:T(8,128)(2,1)}) custom-call(bf16[32,8,1280]{2,1,0:T(8,128)(2,1)S(1)} %all_to_all.36.rows, bf16[256,320]{1,0:T(8,128)(2,1)S(1)} %get-tuple-element.24.grad_before, bf16[256,320]{1,0:T(8,128)(2,1)S(1)} %get-tuple-element.25.after), custom_call_target="tpu_custom_call" | custom-call | tf_op jit(solution)/shard_map/pallas_call | solution.py:16
  118.4 0.0 copy-done.6
  118.4 1.2 shard_map.108
  119.6 9.5 %all-to-all-done.6.got = bf16[8,40,128]{2,1,0:T(8,128)(2,1)S(1)} async-done(((bf16[8,40,128]{2,1,0:T(8,128)(2,1)}), bf16[8,40,128]{2,1,0:T(8,128)(2,1)S(1)}, u32[]{:S(2)}, u32[]{:S(2)}) %all-to-all-start.6) | async-done | bytes 81952 | tf_op jit(solution)/shard_map/all_to_all | solution.py:213
  129.0 0.7 shard_map.110
Async XLA Ops:
  2.4 52.4 %copy-start.5 = (bf16[1,32,320]{2,1,0:T(8,128)(2,1)S(1)}, bf16[1,32,320]{2,1,0:T(8,128)(2,1)}, u32[]{:S(2)}) copy-start(bf16[1,32,320]{2,1,0:T(8,128)(2,1)} %saved.1) | copy-start | bytes 61444
  30.2 24.6 %copy-start.3 = (bf16[1,320,1280]{2,1,0:T(8,128)(2,1)S(1)}, bf16[1,320,1280]{2,1,0:T(8,128)(2,1)}, u32[]{:S(2)}) copy-start(bf16[1,320,1280]{2,1,0:T(8,128)(2,1)} %second.1) | copy-start | bytes 2457604
  30.5 24.4 %copy-start.1 = (bf16[1,576,320]{1,2,0:T(8,128)(2,1)S(1)}, bf16[1,576,320]{1,2,0:T(8,128)(2,1)}, u32[]{:S(2)}) copy-start(bf16[1,576,320]{1,2,0:T(8,128)(2,1)} %param.11) | copy-start | bytes 1105924
  30.5 24.4 %copy-start.2 = (bf16[1,1280,320]{1,2,0:T(8,128)(2,1)S(1)}, bf16[1,1280,320]{1,2,0:T(8,128)(2,1)}, u32[]{:S(2)}) copy-start(bf16[1,1280,320]{1,2,0:T(8,128)(2,1)} %param.12) | copy-start | bytes 2457604
  30.5 24.4 %copy-start.4 = (f32[1,32,576]{2,1,0:T(8,128)S(1)}, f32[1,32,576]{2,1,0:T(8,128)}, u32[]{:S(2)}) copy-start(f32[1,32,576]{2,1,0:T(8,128)} %logits.1) | copy-start | bytes 221188
  69.5 16.0 %copy-start = (bf16[1,576,320]{1,2,0:T(8,128)(2,1)S(1)}, bf16[1,576,320]{1,2,0:T(8,128)(2,1)}, u32[]{:S(2)}) copy-start(bf16[1,576,320]{1,2,0:T(8,128)(2,1)} %param.7) | copy-start | bytes 1105924
  111.8 17.2 %all-to-all-start.6 = ((bf16[8,40,128]{2,1,0:T(8,128)(2,1)}), bf16[8,40,128]{2,1,0:T(8,128)(2,1)S(1)}, u32[]{:S(2)}, u32[]{:S(2)}) async-start(bf16[8,40,128]{2,1,0:T(8,128)(2,1)} %shard_map.109), calls=%async_computation.6 | async-start | bytes 163840 | tf_op jit(solution)/shard_map/all_to_all | solution.py:213
  116.8 1.6 %copy-start.6 = (bf16[320,32]{0,1:T(8,128)(2,1)S(1)}, bf16[320,32]{0,1:T(8,128)(2,1)}, u32[]{:S(2)}) copy-start(bf16[320,32]{0,1:T(8,128)(2,1)} %param.8) | copy-start | bytes 61444

commit v5 on v4

--- a/solution.py
+++ b/solution.py
@@ -8,7 +8,7 @@
 
 F32 = jnp.float32
 BF16 = jnp.bfloat16
-RING = ("zh", "tensor")
+RING = ("tensor", "zh")
 PLANE = ("dp", "y", "core")
 
 
@@ -64,15 +64,15 @@
         ins = slot_in[8 * zh : 8 * zh + 8, :].astype(BF16)
         grads = slot_grad[8 * zh : 8 * zh + 8, :].astype(BF16)
         for zl in range(4):
-            send[4 * zh + zl, :, 0:width] = ins
-            send[4 * zh + zl, :, width : 2 * width] = grads
+            send[zh + 4 * zl, :, 0:width] = ins
+            send[zh + 4 * zl, :, width : 2 * width] = grads
 
 
 def regroup_kernel(got, send, stage):
     width = got.shape[2] // 2
     for zh in range(4):
         for zl in range(4):
-            block = got[4 * zh + zl].astype(F32)
+            block = got[zh + 4 * zl].astype(F32)
             for kind in range(2):
                 row = 32 * kind + 8 * zh
                 stage[row : row + 8, width * zl : width * (zl + 1)] = block[
@@ -99,31 +99,52 @@
     for new, old in pieces():
         combine_term[new : new + 2, :] = term[old : old + 2, :]
     both = rows[...].reshape(256, rows.shape[2])
-    before = rounded_dot(both, first[0], ((1,), (1,)))
-    grad_after = rounded_dot(both, second[0], ((1,), (1,)))
-    grad_after = pltpu.roll(grad_after, 252, 0)
-    is_in = lax.broadcasted_iota(jnp.int32, before.shape, 0) % 8 < 4
+    before = packed(rounded_dot(both, first[0], ((1,), (1,))), 0)
+    grad_after = packed(rounded_dot(both, second[0], ((1,), (1,))), 1)
     square = before * before
     bent = jnp.tanh(GELU_SCALE * (before + GELU_CUBE * (before * square)))
     half = 0.5 * (1.0 + bent)
     slope = half + before * (
         (0.5 * GELU_SCALE) * ((1.0 - bent) * (1.0 + bent)) * (1.0 + (3.0 * GELU_CUBE) * square)
     )
-    grads = jnp.where(is_in, grad_after * slope, 0.0)
-    low = grads.astype(BF16)
-    shifted = pltpu.roll(grads, 4, 0).astype(BF16)
+    low = (grad_after * slope).astype(BF16)
+    grad_before[...] = low
+    after[...] = (before * half).astype(BF16)
     part = first.shape[2] // 2
-    total = jnp.dot(low, first[0, :, :part], preferred_element_type=F32)
-    total = total + jnp.dot(shifted, first[0, :, part:], preferred_element_type=F32)
-    send[...] = total.astype(BF16).reshape(send.shape)
-    grad_before[...] = low
-    after[...] = pltpu.roll(jnp.where(is_in, before * half, 0.0), 4, 0).astype(BF16)
+    left = jnp.dot(low, first[0, :, :part], preferred_element_type=F32)
+    right = jnp.dot(low, first[0, :, part:], preferred_element_type=F32)
+    upper = is_upper(left.shape)
+    send[0:16] = jnp.where(upper, left, pltpu.roll(right, 4, 0)).astype(BF16).reshape(16, 8, part)
+    send[16:32] = jnp.where(upper, pltpu.roll(left, 124, 0), right).astype(BF16).reshape(16, 8, part)
+
+
+def is_upper(dims):
+    return lax.broadcasted_iota(jnp.int32, dims, 0) % 8 < 4
+
+
+def packed(values, kind):
+    head, tail = values[0:128, :], values[128:256, :]
+    if kind == 0:
+        return jnp.where(is_upper(head.shape), head, pltpu.roll(tail, 4, 0))
+    return jnp.where(is_upper(head.shape), pltpu.roll(head, 124, 0), tail)
+
+
+def spread(values, kind):
+    values = values.astype(F32)
+    upper = is_upper(values.shape)
+    if kind == 0:
+        head = jnp.where(upper, values, 0.0)
+        tail = jnp.where(upper, pltpu.roll(values, 124, 0), 0.0)
+    else:
+        head = jnp.where(upper, 0.0, pltpu.roll(values, 4, 0))
+        tail = jnp.where(upper, 0.0, values)
+    return jnp.concatenate([head, tail], axis=0).astype(BF16)
 
 
 def weight_kernel(rows, grad_before, after, grad_first, grad_second):
     both = rows[...].reshape(256, rows.shape[2])
-    grad_first[0] = rounded_dot(grad_before[...], both, ((0,), (0,))).astype(BF16)
-    grad_second[0] = rounded_dot(after[...], both, ((0,), (0,))).astype(BF16)
+    grad_first[0] = rounded_dot(spread(grad_before[...], 0), both, ((0,), (0,))).astype(BF16)
+    grad_second[0] = rounded_dot(spread(after[...], 1), both, ((0,), (0,))).astype(BF16)
 
 
 def partial_kernel(got, send):
@@ -140,14 +161,14 @@
         for zl in range(4):
             at = (zl // 2) * 32 + 8 * zh
             lane = (zl % 2) * width
-            send[4 * zh + zl] = moved[at : at + 8, lane : lane + width]
+            send[zh + 4 * zl] = moved[at : at + 8, lane : lane + width]
 
 
 def back_kernel(got, patches, dispatch, combine_term, send, slot_back):
     for zh in range(4):
-        total = got[4 * zh].astype(F32)
+        total = got[zh].astype(F32)
         for zl in range(1, 4):
-            total = total + got[4 * zh + zl].astype(F32)
+            total = total + got[zh + 4 * zl].astype(F32)
         slot_back[8 * zh : 8 * zh + 8, :] = total
     low = slot_back[...].astype(BF16)
     part = jnp.dot(low, patches[0], preferred_element_type=F32)
@@ -246,8 +267,8 @@
         expert_kernel,
         [
             shape((32, 8, deep // 2), BF16),
-            shape((256, hidden), BF16),
-            shape((256, hidden), BF16),
+            shape((128, hidden), BF16),
+            shape((128, hidden), BF16),
             shape((32, count), F32),
         ],
         rows,

time: 130 us -> 130 us (level)
  no operation moved by 1% of the time
where the time goes in v5:
time: 130 us
  blocking collectives  106 us (82%)
  waiting for transfers between devices  9.44 us (7%)
  Pallas kernels  8.34 us (6%)
  starting transfers between devices  4.82 us (4%)
    all_to_all x6, blocking collectives, exchange(): return lax.all_to_all(value, axes, 0, 0, tiled=True)  106 us
    all_to_all x1, waiting for transfers between devices, exchange(): return lax.all_to_all(value, axes, 0, 0, tiled=True)  9.44 us
    pallas_call x9, Pallas kernels, call(): pl.pallas_call(kernel, out_shape=outs, scratch_shapes=scratch, compiler_p...  6.55 us
    all_to_all x1, starting transfers between devices, exchange(): return lax.all_to_all(value, axes, 0, 0, tiled=True)  4.82 us
  transfers between devices with their start and end apart: 1, of which 1 were waited for; matrix products, arithmetic and copies ran while one was open for 0% of the time, Pallas kernels for 2%

profile of v5, /device:TPU:1, one launch (start us, length us, event | category | flops | bytes accessed | tf_op | source)
XLA Modules:
  0.0 129.7 jit_solution(14951626385862886548)
XLA Ops:
  0.6 1.8 %shard_map.102 = (bf16[16,8,640]{2,1,0:T(8,128)(2,1)S(1)}, f32[32,576]{1,0:T(8,128)S(1)}) custom-call(f32[1,32,576]{2,1,0:T(8,128)} %logits.1, bf16[1,320,576]{2,1,0:T(8,128)(2,1)} %bitcast.7, bf16[1,320,576]{2,1,0:T(8,128)(2,1)} %bitcast.10), custom_call_target="tpu_custom_call" | custom-call | tf_op jit(solution)/shard_map/pallas_call | solution.py:243
  2.4 0.0 copy-start.5
  2.4 27.9 %all_to_all.35.got = bf16[16,8,640]{2,1,0:T(8,128)(2,1)S(1)} all-to-all(bf16[16,8,640]{2,1,0:T(8,128)(2,1)S(1)} %get-tuple-element.17), channel_id=1, replica_groups=mesh['dp'=4,'y'=4,'zh'=4,'core'=2,'tensor'=4] {'tensor','zh'}, dimensions={0} | all-to-all | bytes 327680 | tf_op jit(solution)/shard_map/all_to_all | solution.py:234
  30.3 0.0 copy-start.3
  30.3 0.3 shard_map.103
  30.6 0.0 copy-start.1
  30.6 0.0 copy-start.2
  30.6 0.0 copy-start.4
  30.6 24.0 %all_to_all.36.rows = bf16[32,8,1280]{2,1,0:T(8,128)(2,1)S(1)} all-to-all(bf16[32,8,1280]{2,1,0:T(8,128)(2,1)S(1)} %shard_map.103), channel_id=1, replica_groups=mesh['dp'=4,'y'=4,'zh'=4,'core'=2,'tensor'=4] {'dp','y','core'}, dimensions={0} | all-to-all | bytes 1310720 | tf_op jit(solution)/shard_map/all_to_all | solution.py:234
  54.6 0.0 copy-done.5
  54.6 0.0 copy-done.3
  54.6 0.0 copy-done.1
  54.6 0.0 copy-done.2
  54.6 0.0 copy-done.4
  54.6 1.2 shard_map.104
  55.9 13.2 %all_to_all.37.got = bf16[32,8,640]{2,1,0:T(8,128)(2,1)S(1)} all-to-all(bf16[32,8,640]{2,1,0:T(8,128)(2,1)S(1)} %get-tuple-element.18), channel_id=1, replica_groups=mesh['dp'=4,'y'=4,'zh'=4,'core'=2,'tensor'=4] {'dp','y','core'}, dimensions={0} | all-to-all | bytes 655360 | tf_op jit(solution)/shard_map/all_to_all | solution.py:234
  69.1 0.0 copy-start
  69.1 0.3 shard_map.105
  69.3 16.2 %all_to_all.38.got = bf16[16,8,320]{2,1,0:T(8,128)(2,1)S(1)} all-to-all(bf16[16,8,320]{2,1,0:T(8,128)(2,1)S(1)} %shard_map.105), channel_id=1, replica_groups=mesh['dp'=4,'y'=4,'zh'=4,'core'=2,'tensor'=4] {'tensor','zh'}, dimensions={0} | all-to-all | bytes 163840 | tf_op jit(solution)/shard_map/all_to_all | solution.py:234
  85.5 0.0 copy-done
  85.6 0.3 shard_map.106
  85.8 9.1 %all_to_all.39.got = bf16[4,32,576]{2,1,0:T(8,128)(2,1)S(1)} all-to-all(bf16[4,32,576]{2,1,0:T(8,128)(2,1)S(1)} %get-tuple-element.21), channel_id=1, replica_groups=mesh['dp'=4,'y'=4,'zh'=4,'core'=2,'tensor'=4] {'tensor'}, dimensions={0} | all-to-all | bytes 294912 | tf_op jit(solution)/shard_map/all_to_all | solution.py:234
  95.0 0.3 shard_map.107
  95.3 15.9 %all_to_all.40.got = bf16[32,40,128]{2,1,0:T(8,128)(2,1)S(1)} all-to-all(bf16[32,40,128]{2,1,0:T(8,128)(2,1)S(1)} %get-tuple-element.23), channel_id=1, replica_groups=mesh['dp'=4,'y'=4,'zh'=4,'core'=2,'tensor'=4] {'dp','y','core'}, dimensions={0} | all-to-all | bytes 655360 | tf_op jit(solution)/shard_map/all_to_all | solution.py:234
  111.2 0.7 shard_map.109
  111.9 4.8 %all-to-all-start.6 = ((bf16[8,40,128]{2,1,0:T(8,128)(2,1)}), bf16[8,40,128]{2,1,0:T(8,128)(2,1)S(1)}, u32[]{:S(2)}, u32[]{:S(2)}) async-start(bf16[8,40,128]{2,1,0:T(8,128)(2,1)} %shard_map.109), calls=%async_computation.6 | async-start | bytes 163840 | tf_op jit(solution)/shard_map/all_to_all | solution.py:234
  116.7 0.0 copy-start.6
  116.7 1.6 %shard_map.111 = (bf16[1,320,1280]{2,1,0:T(8,128)(2,1)}, bf16[1,320,1280]{2,1,0:T(8,128)(2,1)}) custom-call(bf16[32,8,1280]{2,1,0:T(8,128)(2,1)S(1)} %all_to_all.36.rows, bf16[128,320]{1,0:T(8,128)(2,1)S(1)} %get-tuple-element.24.grad_before, bf16[128,320]{1,0:T(8,128)(2,1)S(1)} %get-tuple-element.25.after), custom_call_target="tpu_custom_call" | custom-call | tf_op jit(solution)/shard_map/pallas_call | solution.py:16
  118.4 0.0 copy-done.6
  118.4 1.2 shard_map.108
  119.5 9.4 %all-to-all-done.6.got = bf16[8,40,128]{2,1,0:T(8,128)(2,1)S(1)} async-done(((bf16[8,40,128]{2,1,0:T(8,128)(2,1)}), bf16[8,40,128]{2,1,0:T(8,128)(2,1)S(1)}, u32[]{:S(2)}, u32[]{:S(2)}) %all-to-all-start.6) | async-done | bytes 81952 | tf_op jit(solution)/shard_map/all_to_all | solution.py:234
  129.0 0.7 shard_map.110
Async XLA Ops:
  2.4 52.2 %copy-start.5 = (bf16[1,32,320]{2,1,0:T(8,128)(2,1)S(1)}, bf16[1,32,320]{2,1,0:T(8,128)(2,1)}, u32[]{:S(2)}) copy-start(bf16[1,32,320]{2,1,0:T(8,128)(2,1)} %saved.1) | copy-start | bytes 61444
  30.3 24.3 %copy-start.3 = (bf16[1,320,1280]{2,1,0:T(8,128)(2,1)S(1)}, bf16[1,320,1280]{2,1,0:T(8,128)(2,1)}, u32[]{:S(2)}) copy-start(bf16[1,320,1280]{2,1,0:T(8,128)(2,1)} %second.1) | copy-start | bytes 2457604
  30.6 24.0 %copy-start.1 = (bf16[1,576,320]{1,2,0:T(8,128)(2,1)S(1)}, bf16[1,576,320]{1,2,0:T(8,128)(2,1)}, u32[]{:S(2)}) copy-start(bf16[1,576,320]{1,2,0:T(8,128)(2,1)} %param.11) | copy-start | bytes 1105924
  30.6 24.0 %copy-start.2 = (bf16[1,1280,320]{1,2,0:T(8,128)(2,1)S(1)}, bf16[1,1280,320]{1,2,0:T(8,128)(2,1)}, u32[]{:S(2)}) copy-start(bf16[1,1280,320]{1,2,0:T(8,128)(2,1)} %param.12) | copy-start | bytes 2457604
  30.6 24.0 %copy-start.4 = (f32[1,32,576]{2,1,0:T(8,128)S(1)}, f32[1,32,576]{2,1,0:T(8,128)}, u32[]{:S(2)}) copy-start(f32[1,32,576]{2,1,0:T(8,128)} %logits.1) | copy-start | bytes 221188
  69.1 16.5 %copy-start = (bf16[1,576,320]{1,2,0:T(8,128)(2,1)S(1)}, bf16[1,576,320]{1,2,0:T(8,128)(2,1)}, u32[]{:S(2)}) copy-start(bf16[1,576,320]{1,2,0:T(8,128)(2,1)} %param.7) | copy-start | bytes 1105924
  111.9 17.1 %all-to-all-start.6 = ((bf16[8,40,128]{2,1,0:T(8,128)(2,1)}), bf16[8,40,128]{2,1,0:T(8,128)(2,1)S(1)}, u32[]{:S(2)}, u32[]{:S(2)}) async-start(bf16[8,40,128]{2,1,0:T(8,128)(2,1)} %shard_map.109), calls=%async_computation.6 | async-start | bytes 163840 | tf_op jit(solution)/shard_map/all_to_all | solution.py:234
  116.7 1.6 %copy-start.6 = (bf16[320,32]{0,1:T(8,128)(2,1)S(1)}, bf16[320,32]{0,1:T(8,128)(2,1)}, u32[]{:S(2)}) copy-start(bf16[320,32]{0,1:T(8,128)(2,1)} %param.8) | copy-start | bytes 61444

commit v6 on v5

--- a/solution.py
+++ b/solution.py
@@ -8,7 +8,7 @@
 
 F32 = jnp.float32
 BF16 = jnp.bfloat16
-RING = ("tensor", "zh")
+RING = ("zh", "tensor")
 PLANE = ("dp", "y", "core")
 
 
@@ -64,15 +64,15 @@
         ins = slot_in[8 * zh : 8 * zh + 8, :].astype(BF16)
         grads = slot_grad[8 * zh : 8 * zh + 8, :].astype(BF16)
         for zl in range(4):
-            send[zh + 4 * zl, :, 0:width] = ins
-            send[zh + 4 * zl, :, width : 2 * width] = grads
+            send[4 * zh + zl, :, 0:width] = ins
+            send[4 * zh + zl, :, width : 2 * width] = grads
 
 
 def regroup_kernel(got, send, stage):
     width = got.shape[2] // 2
     for zh in range(4):
         for zl in range(4):
-            block = got[zh + 4 * zl].astype(F32)
+            block = got[4 * zh + zl].astype(F32)
             for kind in range(2):
                 row = 32 * kind + 8 * zh
                 stage[row : row + 8, width * zl : width * (zl + 1)] = block[
@@ -161,14 +161,14 @@
         for zl in range(4):
             at = (zl // 2) * 32 + 8 * zh
             lane = (zl % 2) * width
-            send[zh + 4 * zl] = moved[at : at + 8, lane : lane + width]
+            send[4 * zh + zl] = moved[at : at + 8, lane : lane + width]
 
 
 def back_kernel(got, patches, dispatch, combine_term, send, slot_back):
     for zh in range(4):
-        total = got[zh].astype(F32)
+        total = got[4 * zh].astype(F32)
         for zl in range(1, 4):
-            total = total + got[zh + 4 * zl].astype(F32)
+            total = total + got[4 * zh + zl].astype(F32)
         slot_back[8 * zh : 8 * zh + 8, :] = total
     low = slot_back[...].astype(BF16)
     part = jnp.dot(low, patches[0], preferred_element_type=F32)

time: 130 us -> 130 us (level)
  no operation moved by 1% of the time
where the time goes in v6:
time: 130 us; the launch traced here: 129 us
  blocking collectives  106 us (82%)
  waiting for transfers between devices  9.47 us (7%)
  Pallas kernels  8.35 us (6%)
  starting transfers between devices  4.96 us (4%)
    all_to_all x6, blocking collectives, exchange(): return lax.all_to_all(value, axes, 0, 0, tiled=True)  106 us
    all_to_all x1, waiting for transfers between devices, exchange(): return lax.all_to_all(value, axes, 0, 0, tiled=True)  9.47 us
    pallas_call x9, Pallas kernels, call(): pl.pallas_call(kernel, out_shape=outs, scratch_shapes=scratch, compiler_p...  6.56 us
    all_to_all x1, starting transfers between devices, exchange(): return lax.all_to_all(value, axes, 0, 0, tiled=True)  4.96 us
  transfers between devices with their start and end apart: 1, of which 1 were waited for; matrix products, arithmetic and copies ran while one was open for 0% of the time, Pallas kernels for 2%

profile of v6, /device:TPU:1, one launch (start us, length us, event | category | flops | bytes accessed | tf_op | source)
XLA Modules:
  0.0 129.5 jit_solution(3763996001237787549)
XLA Ops:
  0.6 1.8 %shard_map.102 = (bf16[16,8,640]{2,1,0:T(8,128)(2,1)S(1)}, f32[32,576]{1,0:T(8,128)S(1)}) custom-call(f32[1,32,576]{2,1,0:T(8,128)} %logits.1, bf16[1,320,576]{2,1,0:T(8,128)(2,1)} %bitcast.7, bf16[1,320,576]{2,1,0:T(8,128)(2,1)} %bitcast.10), custom_call_target="tpu_custom_call" | custom-call | tf_op jit(solution)/shard_map/pallas_call | solution.py:243
  2.4 0.0 copy-start.5
  2.4 27.8 %all_to_all.35.got = bf16[16,8,640]{2,1,0:T(8,128)(2,1)S(1)} all-to-all(bf16[16,8,640]{2,1,0:T(8,128)(2,1)S(1)} %get-tuple-element.17), channel_id=1, replica_groups=mesh['dp'=4,'y'=4,'zh'=4,'core'=2,'tensor'=4] {'zh','tensor'}, dimensions={0} | all-to-all | bytes 327680 | tf_op jit(solution)/shard_map/all_to_all | solution.py:234
  30.2 0.0 copy-start.3
  30.2 0.3 shard_map.103
  30.5 0.0 copy-start.1
  30.5 0.0 copy-start.2
  30.5 0.0 copy-start.4
  30.5 24.3 %all_to_all.36.rows = bf16[32,8,1280]{2,1,0:T(8,128)(2,1)S(1)} all-to-all(bf16[32,8,1280]{2,1,0:T(8,128)(2,1)S(1)} %shard_map.103), channel_id=1, replica_groups=mesh['dp'=4,'y'=4,'zh'=4,'core'=2,'tensor'=4] {'dp','y','core'}, dimensions={0} | all-to-all | bytes 1310720 | tf_op jit(solution)/shard_map/all_to_all | solution.py:234
  54.8 0.0 copy-done.5
  54.8 0.0 copy-done.3
  54.8 0.0 copy-done.1
  54.8 0.0 copy-done.2
  54.9 0.0 copy-done.4
  54.9 1.2 shard_map.104
  56.1 13.2 %all_to_all.37.got = bf16[32,8,640]{2,1,0:T(8,128)(2,1)S(1)} all-to-all(bf16[32,8,640]{2,1,0:T(8,128)(2,1)S(1)} %get-tuple-element.18), channel_id=1, replica_groups=mesh['dp'=4,'y'=4,'zh'=4,'core'=2,'tensor'=4] {'dp','y','core'}, dimensions={0} | all-to-all | bytes 655360 | tf_op jit(solution)/shard_map/all_to_all | solution.py:234
  69.3 0.0 copy-start
  69.3 0.3 shard_map.105
  69.6 15.7 %all_to_all.38.got = bf16[16,8,320]{2,1,0:T(8,128)(2,1)S(1)} all-to-all(bf16[16,8,320]{2,1,0:T(8,128)(2,1)S(1)} %shard_map.105), channel_id=1, replica_groups=mesh['dp'=4,'y'=4,'zh'=4,'core'=2,'tensor'=4] {'zh','tensor'}, dimensions={0} | all-to-all | bytes 163840 | tf_op jit(solution)/shard_map/all_to_all | solution.py:234
  85.3 0.0 copy-done
  85.3 0.3 shard_map.106
  85.6 9.8 %all_to_all.39.got = bf16[4,32,576]{2,1,0:T(8,128)(2,1)S(1)} all-to-all(bf16[4,32,576]{2,1,0:T(8,128)(2,1)S(1)} %get-tuple-element.21), channel_id=1, replica_groups=mesh['dp'=4,'y'=4,'zh'=4,'core'=2,'tensor'=4] {'tensor'}, dimensions={0} | all-to-all | bytes 294912 | tf_op jit(solution)/shard_map/all_to_all | solution.py:234
  95.3 0.3 shard_map.107
  95.7 15.2 %all_to_all.40.got = bf16[32,40,128]{2,1,0:T(8,128)(2,1)S(1)} all-to-all(bf16[32,40,128]{2,1,0:T(8,128)(2,1)S(1)} %get-tuple-element.23), channel_id=1, replica_groups=mesh['dp'=4,'y'=4,'zh'=4,'core'=2,'tensor'=4] {'dp','y','core'}, dimensions={0} | all-to-all | bytes 655360 | tf_op jit(solution)/shard_map/all_to_all | solution.py:234
  110.9 0.7 shard_map.109
  111.5 5.0 %all-to-all-start.6 = ((bf16[8,40,128]{2,1,0:T(8,128)(2,1)}), bf16[8,40,128]{2,1,0:T(8,128)(2,1)S(1)}, u32[]{:S(2)}, u32[]{:S(2)}) async-start(bf16[8,40,128]{2,1,0:T(8,128)(2,1)} %shard_map.109), calls=%async_computation.6 | async-start | bytes 163840 | tf_op jit(solution)/shard_map/all_to_all | solution.py:234
  116.5 0.0 copy-start.6
  116.5 1.6 %shard_map.111 = (bf16[1,320,1280]{2,1,0:T(8,128)(2,1)}, bf16[1,320,1280]{2,1,0:T(8,128)(2,1)}) custom-call(bf16[32,8,1280]{2,1,0:T(8,128)(2,1)S(1)} %all_to_all.36.rows, bf16[128,320]{1,0:T(8,128)(2,1)S(1)} %get-tuple-element.24.grad_before, bf16[128,320]{1,0:T(8,128)(2,1)S(1)} %get-tuple-element.25.after), custom_call_target="tpu_custom_call" | custom-call | tf_op jit(solution)/shard_map/pallas_call | solution.py:16
  118.1 0.0 copy-done.6
  118.1 1.2 shard_map.108
  119.3 9.5 %all-to-all-done.6.got = bf16[8,40,128]{2,1,0:T(8,128)(2,1)S(1)} async-done(((bf16[8,40,128]{2,1,0:T(8,128)(2,1)}), bf16[8,40,128]{2,1,0:T(8,128)(2,1)S(1)}, u32[]{:S(2)}, u32[]{:S(2)}) %all-to-all-start.6) | async-done | bytes 81952 | tf_op jit(solution)/shard_map/all_to_all | solution.py:234
  128.8 0.7 shard_map.110
Async XLA Ops:
  2.4 52.4 %copy-start.5 = (bf16[1,32,320]{2,1,0:T(8,128)(2,1)S(1)}, bf16[1,32,320]{2,1,0:T(8,128)(2,1)}, u32[]{:S(2)}) copy-start(bf16[1,32,320]{2,1,0:T(8,128)(2,1)} %saved.1) | copy-start | bytes 61444
  30.2 24.6 %copy-start.3 = (bf16[1,320,1280]{2,1,0:T(8,128)(2,1)S(1)}, bf16[1,320,1280]{2,1,0:T(8,128)(2,1)}, u32[]{:S(2)}) copy-start(bf16[1,320,1280]{2,1,0:T(8,128)(2,1)} %second.1) | copy-start | bytes 2457604
  30.5 24.4 %copy-start.1 = (bf16[1,576,320]{1,2,0:T(8,128)(2,1)S(1)}, bf16[1,576,320]{1,2,0:T(8,128)(2,1)}, u32[]{:S(2)}) copy-start(bf16[1,576,320]{1,2,0:T(8,128)(2,1)} %param.11) | copy-start | bytes 1105924
  30.5 24.4 %copy-start.2 = (bf16[1,1280,320]{1,2,0:T(8,128)(2,1)S(1)}, bf16[1,1280,320]{1,2,0:T(8,128)(2,1)}, u32[]{:S(2)}) copy-start(bf16[1,1280,320]{1,2,0:T(8,128)(2,1)} %param.12) | copy-start | bytes 2457604
  30.5 24.4 %copy-start.4 = (f32[1,32,576]{2,1,0:T(8,128)S(1)}, f32[1,32,576]{2,1,0:T(8,128)}, u32[]{:S(2)}) copy-start(f32[1,32,576]{2,1,0:T(8,128)} %logits.1) | copy-start | bytes 221188
  69.3 16.0 %copy-start = (bf16[1,576,320]{1,2,0:T(8,128)(2,1)S(1)}, bf16[1,576,320]{1,2,0:T(8,128)(2,1)}, u32[]{:S(2)}) copy-start(bf16[1,576,320]{1,2,0:T(8,128)(2,1)} %param.7) | copy-start | bytes 1105924
  111.5 17.2 %all-to-all-start.6 = ((bf16[8,40,128]{2,1,0:T(8,128)(2,1)}), bf16[8,40,128]{2,1,0:T(8,128)(2,1)S(1)}, u32[]{:S(2)}, u32[]{:S(2)}) async-start(bf16[8,40,128]{2,1,0:T(8,128)(2,1)} %shard_map.109), calls=%async_computation.6 | async-start | bytes 163840 | tf_op jit(solution)/shard_map/all_to_all | solution.py:234
  116.5 1.6 %copy-start.6 = (bf16[320,32]{0,1:T(8,128)(2,1)S(1)}, bf16[320,32]{0,1:T(8,128)(2,1)}, u32[]{:S(2)}) copy-start(bf16[320,32]{0,1:T(8,128)(2,1)} %param.8) | copy-start | bytes 61444

commit v7 on v6

--- a/solution.py
+++ b/solution.py
@@ -174,16 +174,22 @@
     part = jnp.dot(low, patches[0], preferred_element_type=F32)
     by_patch = dispatch[...]
     grads = by_patch * (part - jnp.sum(by_patch * part, axis=1, keepdims=True))
-    grads = (grads + combine_term[...]).astype(BF16)
+    grads = grads + combine_term[...]
+    rest = jnp.concatenate([grads[0:16, 512:], grads[16:32, 512:]], axis=1).astype(BF16)
+    grads = grads.astype(BF16)
     for zl in range(4):
-        send[zl] = grads
+        for k in range(4):
+            send[zl, 32 * k : 32 * k + 32, :] = grads[:, 128 * k : 128 * k + 128]
+        send[zl, 128:144, :] = rest
 
 
 def logit_kernel(got, patches, grad_logits, send, stage):
     total = got[0].astype(F32)
     for zl in range(1, 4):
         total = total + got[zl].astype(F32)
-    low = total.astype(BF16)
+    rest = jnp.concatenate([total[128:144, 0:64], total[128:144, 64:128]], axis=0)
+    blocks = [total[32 * k : 32 * k + 32, :] for k in range(4)]
+    low = jnp.concatenate(blocks + [rest], axis=1).astype(BF16)
     grad_logits[...] = low
     router = rounded_dot(low, patches[0], ((1,), (1,)))
     for new, old in pieces():
@@ -290,7 +296,7 @@
     got = exchange(send, RING)
     send, slot_back = call(
         back_kernel,
-        [shape((4, 32, count), BF16), shape((32, width), F32)],
+        [shape((4, 144, 128), BF16), shape((32, width), F32)],
         got,
         patches,
         dispatch,

time: 130 us -> 130 us (level)
  no operation moved by 1% of the time
where the time goes in v7:
time: 130 us; the launch traced here: 129 us
  blocking collectives  106 us (82%)
  waiting for transfers between devices  9.48 us (7%)
  Pallas kernels  8.42 us (6%)
  starting transfers between devices  4.96 us (4%)
    all_to_all x6, blocking collectives, exchange(): return lax.all_to_all(value, axes, 0, 0, tiled=True)  106 us
    all_to_all x1, waiting for transfers between devices, exchange(): return lax.all_to_all(value, axes, 0, 0, tiled=True)  9.48 us
    pallas_call x9, Pallas kernels, call(): pl.pallas_call(kernel, out_shape=outs, scratch_shapes=scratch, compiler_p...  6.63 us
    all_to_all x1, starting transfers between devices, exchange(): return lax.all_to_all(value, axes, 0, 0, tiled=True)  4.96 us
  transfers between devices with their start and end apart: 1, of which 1 were waited for; matrix products, arithmetic and copies ran while one was open for 0% of the time, Pallas kernels for 2%

profile of v7, /device:TPU:1, one launch (start us, length us, event | category | flops | bytes accessed | tf_op | source)
XLA Modules:
  0.0 129.5 jit_solution(17140232509156664341)
XLA Ops:
  0.6 1.8 %shard_map.102 = (bf16[16,8,640]{2,1,0:T(8,128)(2,1)S(1)}, f32[32,576]{1,0:T(8,128)S(1)}) custom-call(f32[1,32,576]{2,1,0:T(8,128)} %logits.1, bf16[1,320,576]{2,1,0:T(8,128)(2,1)} %bitcast.7, bf16[1,320,576]{2,1,0:T(8,128)(2,1)} %bitcast.10), custom_call_target="tpu_custom_call" | custom-call | tf_op jit(solution)/shard_map/pallas_call | solution.py:249
  2.4 0.0 copy-start.5
  2.4 27.8 %all_to_all.35.got = bf16[16,8,640]{2,1,0:T(8,128)(2,1)S(1)} all-to-all(bf16[16,8,640]{2,1,0:T(8,128)(2,1)S(1)} %get-tuple-element.17), channel_id=1, replica_groups=mesh['dp'=4,'y'=4,'zh'=4,'core'=2,'tensor'=4] {'zh','tensor'}, dimensions={0} | all-to-all | bytes 327680 | tf_op jit(solution)/shard_map/all_to_all | solution.py:240
  30.2 0.0 copy-start.3
  30.2 0.3 shard_map.103
  30.5 0.0 copy-start.1
  30.5 0.0 copy-start.2
  30.5 0.0 copy-start.4
  30.5 24.3 %all_to_all.36.rows = bf16[32,8,1280]{2,1,0:T(8,128)(2,1)S(1)} all-to-all(bf16[32,8,1280]{2,1,0:T(8,128)(2,1)S(1)} %shard_map.103), channel_id=1, replica_groups=mesh['dp'=4,'y'=4,'zh'=4,'core'=2,'tensor'=4] {'dp','y','core'}, dimensions={0} | all-to-all | bytes 1310720 | tf_op jit(solution)/shard_map/all_to_all | solution.py:240
  54.8 0.0 copy-done.5
  54.8 0.0 copy-done.3
  54.8 0.0 copy-done.1
  54.8 0.0 copy-done.2
  54.9 0.0 copy-done.4
  54.9 1.2 shard_map.104
  56.1 13.2 %all_to_all.37.got = bf16[32,8,640]{2,1,0:T(8,128)(2,1)S(1)} all-to-all(bf16[32,8,640]{2,1,0:T(8,128)(2,1)S(1)} %get-tuple-element.18), channel_id=1, replica_groups=mesh['dp'=4,'y'=4,'zh'=4,'core'=2,'tensor'=4] {'dp','y','core'}, dimensions={0} | all-to-all | bytes 655360 | tf_op jit(solution)/shard_map/all_to_all | solution.py:240
  69.3 0.0 copy-start
  69.3 0.3 shard_map.105
  69.6 15.7 %all_to_all.38.got = bf16[16,8,320]{2,1,0:T(8,128)(2,1)S(1)} all-to-all(bf16[16,8,320]{2,1,0:T(8,128)(2,1)S(1)} %shard_map.105), channel_id=1, replica_groups=mesh['dp'=4,'y'=4,'zh'=4,'core'=2,'tensor'=4] {'zh','tensor'}, dimensions={0} | all-to-all | bytes 163840 | tf_op jit(solution)/shard_map/all_to_all | solution.py:240
  85.3 0.0 copy-done
  85.3 0.3 shard_map.106
  85.6 9.7 %all_to_all.39.got = bf16[4,144,128]{2,1,0:T(8,128)(2,1)S(1)} all-to-all(bf16[4,144,128]{2,1,0:T(8,128)(2,1)S(1)} %get-tuple-element.21), channel_id=1, replica_groups=mesh['dp'=4,'y'=4,'zh'=4,'core'=2,'tensor'=4] {'tensor'}, dimensions={0} | all-to-all | bytes 294912 | tf_op jit(solution)/shard_map/all_to_all | solution.py:240
  95.3 0.3 shard_map.107
  95.7 15.2 %all_to_all.40.got = bf16[32,40,128]{2,1,0:T(8,128)(2,1)S(1)} all-to-all(bf16[32,40,128]{2,1,0:T(8,128)(2,1)S(1)} %get-tuple-element.23), channel_id=1, replica_groups=mesh['dp'=4,'y'=4,'zh'=4,'core'=2,'tensor'=4] {'dp','y','core'}, dimensions={0} | all-to-all | bytes 655360 | tf_op jit(solution)/shard_map/all_to_all | solution.py:240
  110.9 0.7 shard_map.109
  111.6 5.0 %all-to-all-start.6 = ((bf16[8,40,128]{2,1,0:T(8,128)(2,1)}), bf16[8,40,128]{2,1,0:T(8,128)(2,1)S(1)}, u32[]{:S(2)}, u32[]{:S(2)}) async-start(bf16[8,40,128]{2,1,0:T(8,128)(2,1)} %shard_map.109), calls=%async_computation.6 | async-start | bytes 163840 | tf_op jit(solution)/shard_map/all_to_all | solution.py:240
  116.5 0.0 copy-start.6
  116.5 1.6 %shard_map.111 = (bf16[1,320,1280]{2,1,0:T(8,128)(2,1)}, bf16[1,320,1280]{2,1,0:T(8,128)(2,1)}) custom-call(bf16[32,8,1280]{2,1,0:T(8,128)(2,1)S(1)} %all_to_all.36.rows, bf16[128,320]{1,0:T(8,128)(2,1)S(1)} %get-tuple-element.24.grad_before, bf16[128,320]{1,0:T(8,128)(2,1)S(1)} %get-tuple-element.25.after), custom_call_target="tpu_custom_call" | custom-call | tf_op jit(solution)/shard_map/pallas_call | solution.py:16
  118.1 0.0 copy-done.6
  118.1 1.2 shard_map.108
  119.3 9.5 %all-to-all-done.6.got = bf16[8,40,128]{2,1,0:T(8,128)(2,1)S(1)} async-done(((bf16[8,40,128]{2,1,0:T(8,128)(2,1)}), bf16[8,40,128]{2,1,0:T(8,128)(2,1)S(1)}, u32[]{:S(2)}, u32[]{:S(2)}) %all-to-all-start.6) | async-done | bytes 81952 | tf_op jit(solution)/shard_map/all_to_all | solution.py:240
  128.8 0.7 shard_map.110
Async XLA Ops:
  2.4 52.4 %copy-start.5 = (bf16[1,32,320]{2,1,0:T(8,128)(2,1)S(1)}, bf16[1,32,320]{2,1,0:T(8,128)(2,1)}, u32[]{:S(2)}) copy-start(bf16[1,32,320]{2,1,0:T(8,128)(2,1)} %saved.1) | copy-start | bytes 61444
  30.2 24.6 %copy-start.3 = (bf16[1,320,1280]{2,1,0:T(8,128)(2,1)S(1)}, bf16[1,320,1280]{2,1,0:T(8,128)(2,1)}, u32[]{:S(2)}) copy-start(bf16[1,320,1280]{2,1,0:T(8,128)(2,1)} %second.1) | copy-start | bytes 2457604
  30.5 24.4 %copy-start.1 = (bf16[1,576,320]{1,2,0:T(8,128)(2,1)S(1)}, bf16[1,576,320]{1,2,0:T(8,128)(2,1)}, u32[]{:S(2)}) copy-start(bf16[1,576,320]{1,2,0:T(8,128)(2,1)} %param.11) | copy-start | bytes 1105924
  30.5 24.4 %copy-start.2 = (bf16[1,1280,320]{1,2,0:T(8,128)(2,1)S(1)}, bf16[1,1280,320]{1,2,0:T(8,128)(2,1)}, u32[]{:S(2)}) copy-start(bf16[1,1280,320]{1,2,0:T(8,128)(2,1)} %param.12) | copy-start | bytes 2457604
  30.5 24.4 %copy-start.4 = (f32[1,32,576]{2,1,0:T(8,128)S(1)}, f32[1,32,576]{2,1,0:T(8,128)}, u32[]{:S(2)}) copy-start(f32[1,32,576]{2,1,0:T(8,128)} %logits.1) | copy-start | bytes 221188
  69.3 16.0 %copy-start = (bf16[1,576,320]{1,2,0:T(8,128)(2,1)S(1)}, bf16[1,576,320]{1,2,0:T(8,128)(2,1)}, u32[]{:S(2)}) copy-start(bf16[1,576,320]{1,2,0:T(8,128)(2,1)} %param.7) | copy-start | bytes 1105924
  111.6 17.2 %all-to-all-start.6 = ((bf16[8,40,128]{2,1,0:T(8,128)(2,1)}), bf16[8,40,128]{2,1,0:T(8,128)(2,1)S(1)}, u32[]{:S(2)}, u32[]{:S(2)}) async-start(bf16[8,40,128]{2,1,0:T(8,128)(2,1)} %shard_map.109), calls=%async_computation.6 | async-start | bytes 163840 | tf_op jit(solution)/shard_map/all_to_all | solution.py:240
  116.5 1.6 %copy-start.6 = (bf16[320,32]{0,1:T(8,128)(2,1)S(1)}, bf16[320,32]{0,1:T(8,128)(2,1)}, u32[]{:S(2)}) copy-start(bf16[320,32]{0,1:T(8,128)(2,1)} %param.8) | copy-start | bytes 61444
